TPU v7x, 32 devices: a whole 2x2x4 slice. The times are simulated.
32 devices in a mesh: dp: 8 (over z, x), tensor: 4 (over y, core).
Axes of the slice: x: 2, y: 2, z: 4, core: 2. Of those that a mesh axis runs over, the one named last changes fastest.
Arguments:
- hidden_in: bfloat16 [8192, 2048], P('dp', 'tensor'), may hold values from -6 to 6
- norm1_gain: bfloat16 [2048], replicated, may hold values from 0.5 to 1.5
- w_query: bfloat16 [2048, 2048], P(None, 'tensor'), may hold values from -0.125 to 0.125
- w_key: bfloat16 [2048, 2048], P(None, 'tensor'), may hold values from -0.125 to 0.125
- w_value: bfloat16 [2048, 2048], P(None, 'tensor'), may hold values from -0.125 to 0.125
- w_out: bfloat16 [2048, 2048], P('tensor'), may hold values from -1 to 1
- norm2_gain: bfloat16 [2048], replicated, may hold values from 0.5 to 1.5
- w_gate: bfloat16 [2048, 8192], P(None, 'tensor'), may hold values from -0.125 to 0.125
- w_up: bfloat16 [2048, 8192], P(None, 'tensor'), may hold values from -0.125 to 0.125
- w_down: bfloat16 [8192, 2048], P('tensor'), may hold values from -0.125 to 0.125
- tile_len: int32 [64], P('dp'), may hold values from 0 to 128, as said below
- tile_offset: int32 [64], P('dp'), may hold values from 0 to 7, as said below
- cotangent: bfloat16 [8192, 2048], P('dp', 'tensor'), may hold values from -6 to 6
Outputs:
- layer_out: bfloat16 [8192, 2048], P('dp', 'tensor')
- input_grad: bfloat16 [8192, 2048], P('dp', 'tensor')
- norm1_gain_grad: float32 [2048], P('dp')
- w_query_grad: float32 [2048, 2048], P('dp', 'tensor')
- w_key_grad: float32 [2048, 2048], P('dp', 'tensor')
- w_value_grad: float32 [2048, 2048], P('dp', 'tensor')
- w_out_grad: float32 [2048, 2048], P('tensor', 'dp')
- norm2_gain_grad: float32 [2048], P('dp')
- w_gate_grad: float32 [2048, 8192], P('dp', 'tensor')
- w_up_grad: float32 [2048, 8192], P('dp', 'tensor')
- w_down_grad: float32 [8192, 2048], P('tensor', 'dp')
Inputs may be any that keep to these rules, and one draw needn't show every extreme that they name: `tile_len`: each slot block of 8 tiles holds whole sequences in order, each beginning at a tile with offset 0; a tile with offset k > 0 continues the sequence of the tile before it, which then holds 128 tokens; a tile's tokens fill its first rows; tiles without tokens come last in a block and have offset 0; some block holds a sequence of 1024 tokens. `tile_offset`: A sequence spans at most 8 tiles.
All inputs are finite; a program needn't handle non-finite values.
Results may differ from a plain program's by a relative error of at most 0.015.
Values may be sent and summed in bfloat16 or wider, within the bound.
A program may use at most 320 MiB of HBM per device.

v0:
```python
import jax
import jax.numpy as jnp
from jax import lax
from jax.sharding import PartitionSpec as P

HD = 64
TILE = 128


def rms_scale(values):
    return lax.rsqrt(jnp.mean(values * values, axis=1, keepdims=True) + 1e-05)


def norm_back(values, inv_rms, gain_vec, upstream):
    gained = upstream * gain_vec
    gain_grad = jnp.sum(upstream * values * inv_rms, axis=0)
    inner = jnp.mean(gained * values, axis=1, keepdims=True)
    return (inv_rms * gained - values * (inv_rms * inv_rms * inv_rms) * inner, gain_grad)


def rotate(values, cosine_tab, sine_tab):
    half_width = values.shape[-1] // 2
    lower_half = values[..., :half_width]
    upper_half = values[..., half_width:]
    return jnp.concatenate(
        [
            lower_half * cosine_tab - upper_half * sine_tab,
            upper_half * cosine_tab + lower_half * sine_tab,
        ],
        axis=-1,
    )


def unrotate(grads, cosine_tab, sine_tab):
    half_width = grads.shape[-1] // 2
    lower_half = grads[..., :half_width]
    upper_half = grads[..., half_width:]
    return jnp.concatenate(
        [
            lower_half * cosine_tab + upper_half * sine_tab,
            upper_half * cosine_tab - lower_half * sine_tab,
        ],
        axis=-1,
    )


def rope_tables(position):
    frequency = jnp.power(130000.0, -2.0 * jnp.arange(HD // 2, dtype=jnp.float32) / HD)
    angles = position[:, None] * frequency[None, :]
    return (jnp.cos(angles)[:, None, :], jnp.sin(angles)[:, None, :])


def row_layout(tile_len, tile_offset):
    tile_count = tile_len.shape[0]
    within = jnp.tile(jnp.arange(TILE, dtype=jnp.int32), tile_count)
    lengths = jnp.repeat(tile_len, TILE)
    starts = jnp.repeat(tile_offset, TILE)
    sequence = jnp.repeat(jnp.cumsum((tile_offset == 0).astype(jnp.int32)), TILE)
    live_rows = (within < lengths).astype(jnp.float32)
    position = (starts * TILE + within).astype(jnp.float32)
    slot_ids = jnp.arange(tile_count * TILE, dtype=jnp.int32)
    allowed = (sequence[:, None] == sequence[None, :]) & (
        slot_ids[None, :] <= slot_ids[:, None]
    ) & (live_rows[None, :] > 0) | (slot_ids[:, None] == slot_ids[None, :])
    return (live_rows[:, None], position, allowed)


def contract_rows(left_op, right_op):
    return lax.dot_general(
        left_op, right_op, (((0,), (0,)), ((), ())), preferred_element_type=jnp.float32
    )


def times_transposed(left_op, right_op):
    return lax.dot_general(
        left_op, right_op, (((1,), (1,)), ((), ())), preferred_element_type=jnp.float32
    )


def attention_scores(query_rot, key_rot, allowed):
    raw_scores = 0.125 * jnp.einsum(
        "qhd,khd->hqk", query_rot, key_rot, preferred_element_type=jnp.float32
    )
    return jnp.where(allowed[None], raw_scores, -1000000000.0)


def own_cols(values, own_start, own_width):
    return lax.dynamic_slice_in_dim(values, own_start, own_width, 1)


def shards(
    hidden_in,
    norm1_gain,
    w_query,
    w_key,
    w_value,
    w_out,
    norm2_gain,
    w_gate,
    w_up,
    w_down,
    tile_len,
    tile_offset,
    cotangent,
):
    inputs_bf, cot_bf = (
        lax.all_gather(hidden_in, "tensor", axis=1, tiled=True),
        lax.all_gather(cotangent, "tensor", axis=1, tiled=True),
    )
    slot_count = inputs_bf.shape[0]
    full_width = inputs_bf.shape[1]
    own_width = full_width // lax.axis_size("tensor")
    own_start = lax.axis_index("tensor") * own_width
    live_rows, position, allowed = row_layout(tile_len, tile_offset)
    cosine_tab, sine_tab = rope_tables(position)
    row_vals = inputs_bf.astype(jnp.float32)
    gain_one = norm1_gain.astype(jnp.float32)
    gain_two = norm2_gain.astype(jnp.float32)
    head_count = w_query.shape[1] // HD
    inv_one = rms_scale(row_vals)
    normed_one = (row_vals * inv_one * gain_one).astype(jnp.bfloat16)
    query_raw = jnp.dot(normed_one, w_query, preferred_element_type=jnp.float32).reshape(
        slot_count, head_count, HD
    )
    key_raw = jnp.dot(normed_one, w_key, preferred_element_type=jnp.float32).reshape(
        slot_count, head_count, HD
    )
    value_bf = (
        jnp.dot(normed_one, w_value, preferred_element_type=jnp.float32)
        .astype(jnp.bfloat16)
        .reshape(slot_count, head_count, HD)
    )
    query_rot = rotate(query_raw, cosine_tab, sine_tab).astype(jnp.bfloat16)
    key_rot = rotate(key_raw, cosine_tab, sine_tab).astype(jnp.bfloat16)
    scores = attention_scores(query_rot, key_rot, allowed)
    row_top = jnp.max(scores, axis=2, keepdims=True)
    log_total = row_top + jnp.log(jnp.sum(jnp.exp(scores - row_top), axis=2, keepdims=True))
    attn_probs = jnp.exp(scores - log_total)
    mixed = jnp.einsum(
        "hqk,khd->qhd",
        attn_probs.astype(jnp.bfloat16),
        value_bf,
        preferred_element_type=jnp.float32,
    )
    attended = mixed.reshape(slot_count, head_count * HD).astype(jnp.bfloat16)
    attn_sum = lax.psum(jnp.dot(attended, w_out, preferred_element_type=jnp.float32), "tensor")
    resid = row_vals + live_rows * attn_sum
    inv_two = rms_scale(resid)
    normed_two = (resid * inv_two * gain_two).astype(jnp.bfloat16)
    gate_pre = jnp.dot(normed_two, w_gate, preferred_element_type=jnp.float32)
    up_pre = jnp.dot(normed_two, w_up, preferred_element_type=jnp.float32)
    sigmoid_gate = jax.nn.sigmoid(gate_pre)
    silu_gate = gate_pre * sigmoid_gate
    hidden = (silu_gate * up_pre).astype(jnp.bfloat16)
    mlp_term = jnp.dot(hidden, w_down, preferred_element_type=jnp.float32)
    mlp_sum = lax.psum(mlp_term.astype(jnp.bfloat16), "tensor").astype(jnp.float32)
    layer_out = own_cols(resid + live_rows * mlp_sum, own_start, own_width).astype(jnp.bfloat16)
    upstream = cot_bf.astype(jnp.float32)
    d_mlp = (live_rows * upstream).astype(jnp.bfloat16)
    grad_down = contract_rows(hidden, d_mlp)
    d_hidden = times_transposed(d_mlp, w_down)
    d_gate = (d_hidden * up_pre * sigmoid_gate * (1.0 + gate_pre * (1.0 - sigmoid_gate))).astype(
        jnp.bfloat16
    )
    d_up = (d_hidden * silu_gate).astype(jnp.bfloat16)
    grad_gate = contract_rows(normed_two, d_gate)
    grad_up = contract_rows(normed_two, d_up)
    d_norm_two = lax.psum(times_transposed(d_gate, w_gate) + times_transposed(d_up, w_up), "tensor")
    d_resid_norm, grad_gain_two = norm_back(resid, inv_two, gain_two, d_norm_two)
    d_resid = upstream + d_resid_norm
    d_attn = (live_rows * d_resid).astype(jnp.bfloat16)
    grad_out = contract_rows(attended, d_attn)
    d_attended = (
        times_transposed(d_attn, w_out).astype(jnp.bfloat16).reshape(slot_count, head_count, HD)
    )
    again_probs = jnp.exp(attention_scores(query_rot, key_rot, allowed) - log_total)
    d_value = jnp.einsum(
        "hqk,qhd->khd",
        again_probs.astype(jnp.bfloat16),
        d_attended,
        preferred_element_type=jnp.float32,
    )
    d_value = d_value.astype(jnp.bfloat16).reshape(slot_count, head_count * HD)
    d_probs = jnp.einsum("qhd,khd->hqk", d_attended, value_bf, preferred_element_type=jnp.float32)
    d_scores = (
        again_probs * (d_probs - jnp.sum(again_probs * d_probs, axis=2, keepdims=True))
    ).astype(jnp.bfloat16)
    d_query_rot = 0.125 * jnp.einsum(
        "hqk,khd->qhd", d_scores, key_rot, preferred_element_type=jnp.float32
    )
    d_key_rot = 0.125 * jnp.einsum(
        "hqk,qhd->khd", d_scores, query_rot, preferred_element_type=jnp.float32
    )
    d_query = (
        unrotate(d_query_rot, cosine_tab, sine_tab)
        .astype(jnp.bfloat16)
        .reshape(slot_count, head_count * HD)
    )
    d_key = (
        unrotate(d_key_rot, cosine_tab, sine_tab)
        .astype(jnp.bfloat16)
        .reshape(slot_count, head_count * HD)
    )
    grad_query = contract_rows(normed_one, d_query)
    grad_key = contract_rows(normed_one, d_key)
    grad_value = contract_rows(normed_one, d_value)
    d_norm_part = (
        times_transposed(d_query, w_query)
        + times_transposed(d_key, w_key)
        + times_transposed(d_value, w_value)
    )
    d_norm_one = lax.psum(d_norm_part, "tensor")
    d_input_norm, grad_gain_one = norm_back(row_vals, inv_one, gain_one, d_norm_one)
    input_grad = own_cols(d_resid + d_input_norm, own_start, own_width).astype(jnp.bfloat16)
    all_sums = (
        lax.psum_scatter(grad_query, "dp", scatter_dimension=0, tiled=True),
        lax.psum_scatter(grad_key, "dp", scatter_dimension=0, tiled=True),
        lax.psum_scatter(grad_value, "dp", scatter_dimension=0, tiled=True),
        lax.psum_scatter(grad_out, "dp", scatter_dimension=1, tiled=True),
        lax.psum_scatter(grad_gate, "dp", scatter_dimension=0, tiled=True),
        lax.psum_scatter(grad_up, "dp", scatter_dimension=0, tiled=True),
        lax.psum_scatter(grad_down, "dp", scatter_dimension=1, tiled=True),
        lax.psum_scatter(grad_gain_one, "dp", scatter_dimension=0, tiled=True),
        lax.psum_scatter(grad_gain_two, "dp", scatter_dimension=0, tiled=True),
    )
    (
        sum_query,
        sum_key,
        sum_value,
        sum_out,
        sum_gate,
        sum_up,
        sum_down,
        sum_gain_one,
        sum_gain_two,
    ) = all_sums
    return (
        layer_out,
        input_grad,
        sum_gain_one,
        sum_query,
        sum_key,
        sum_value,
        sum_out,
        sum_gain_two,
        sum_gate,
        sum_up,
        sum_down,
    )


def solution(mesh):
    in_specs = (
        P("dp", "tensor"),
        P(),
        P(None, "tensor"),
        P(None, "tensor"),
        P(None, "tensor"),
        P("tensor", None),
        P(),
        P(None, "tensor"),
        P(None, "tensor"),
        P("tensor", None),
        P("dp"),
        P("dp"),
        P("dp", "tensor"),
    )
    out_specs = (
        P("dp", "tensor"),
        P("dp", "tensor"),
        P("dp"),
        P("dp", "tensor"),
        P("dp", "tensor"),
        P("dp", "tensor"),
        P("tensor", "dp"),
        P("dp"),
        P("dp", "tensor"),
        P("dp", "tensor"),
        P("tensor", "dp"),
    )
    return jax.shard_map(shards, mesh=mesh, in_specs=in_specs, out_specs=out_specs, check_vma=False)
```

profile of v0, /device:TPU:0, one launch (start us, length us, event | category | flops | bytes accessed | tf_op | source)
XLA Modules:
  0.0 2016.1 jit_solution(10223739987469620395)
XLA Ops:
  13.6 33.2 %all-gather.3.cloned.1.call-done = bf16[1024,2048]{1,0:T(8,128)(2,1)} async-done(((bf16[1024,512]{1,0:T(8,128)(2,1)}), bf16[1024,2048]{1,0:T(8,128)(2,1)}) %all-gather.3.cloned.1.call-update) | async-done | bytes 4194320 | tf_op jit(solution)/shard_map/all_gather | solution.py:107
  46.8 3.1 fusion.2
  50.5 5.5 fusion.37
  56.0 2.6 fusion.35
  60.2 15.1 fusion
  75.4 14.8 exponential_reduce_fusion
  90.3 2.5 convolution_convert_fusion.4
  92.8 15.2 convolution_convert_fusion.3
  109.0 5.6 fusion.40
  115.6 152.1 %all-reduce.8.cloned.1.call-done = f32[1024,2048]{1,0:T(8,128)} async-done(((f32[1024,2048]{1,0:T(8,128)}), f32[1024,2048]{1,0:T(8,128)}) %all-reduce.8.cloned.1.call-update) | async-done | bytes 8388624 | tf_op jit(solution)/shard_map/psum | solution.py:146
  267.7 5.7 multiply_reduce_fusion.3
  274.3 16.6 fusion.42
  290.9 13.4 fusion.41
  304.3 22.0 %multiply_convert_fusion.2 = (bf16[1024,2048]{1,0:T(8,128)(2,1)}, bf16[1024,2048]{1,0:T(8,128)(2,1)}, bf16[1024,2048]{1,0:T(8,128)(2,1)}) fusion(f32[1024,2048]{1,0:T(8,128)} %fusion.41, f32[1024,2048]{1,0:T(8,128)} %fusion.42, bf16[2048,2048]{1,0:T(8,128)(2,1)} %param.22, bf16[1024,2048]{1,0:T(8,128)(2,1)} %all-gather.5.cloned.1.call-done, ...), kind=kOutput, calls=%fused_computation.25 | convolution fusion | flops 8627683328 | bytes 41947136 | tf_op jit(solution)/shard_map/dot_general | solution.py:75
  326.3 12.7 fusion.43
  339.0 13.8 convolution_add_fusion
  352.8 13.9 convolution_convert_fusion
  366.8 139.1 %all-reduce.12.cloned.1.call-done = f32[1024,2048]{1,0:T(8,128)} async-done(((f32[1024,2048]{1,0:T(8,128)}), f32[1024,2048]{1,0:T(8,128)}) %all-reduce.12.cloned.1.call-update) | async-done | bytes 8388624 | tf_op jit(solution)/shard_map/psum | solution.py:168
  505.9 8.3 multiply_reduce_fusion.1
  516.0 4.7 convert_add_fusion
  520.8 3.7 convolution_convert_fusion.2
  524.5 16.3 convolution_convert_fusion.1
  540.8 24.1 %multiply_reduce_fusion = (f32[8,1024]{1,0:T(8,128)S(1)}, f32[8,1024,1024]{1,2,0:T(8,128)}) fusion(f32[8,1024,1024]{1,2,0:T(8,128)} %get-tuple-element.42, f32[8,1024]{1,0:T(8,128)S(1)} %copy-done.17, pred[1024,1024]{0,1:T(8,128)(4,1)S(1)} %copy-done.6, bf16[1024,8,64]{0,2,1:T(8,128)(2,1)S(1)} %bitcast.71, bf16[1024,8,64]{0,2,1:T(8,128)(2,1)S(1)} %bitcast.69), kind=kOutput, calls=%fused_computation.1 | convolution fusion | flops 1115676672 | bytes 70320128 | tf_op jit(solution)/shard_map/qhd,khd->hqk/dot_general | solution.py:184
  564.9 28.8 %multiply_convert_fusion = bf16[8,1024,1024]{1,2,0:T(8,128)(2,1)} fusion(f32[8,1024,1024]{1,2,0:T(8,128)} %get-tuple-element.44, f32[8,1024,1024]{1,2,0:T(8,128)} %get-tuple-element.42, f32[8,1024]{1,0:T(8,128)S(1)} %get-tuple-element.43, f32[8,1024]{1,0:T(8,128)S(1)} %copy-done.17, pred[1024,1024]{0,1:T(8,128)(4,1)S(1)} %copy-done.6), kind=kLoop, calls=%fused_computation | loop fusion | flops 50331648 | bytes 85000192 | tf_op jit(solution)/shard_map/convert_element_type | solution.py:187
  593.8 11.4 multiply_bitcast_fusion
  605.2 8.8 multiply_bitcast_fusion.1
  615.9 2.4 fusion.44
  620.8 6.0 add_add_fusion
  628.1 7.8 fusion.28
  636.0 6.9 fusion.29
  643.0 7.1 fusion.31
  650.2 6.9 fusion.33
  657.2 15.9 fusion.17
  673.2 15.3 fusion.47
  688.6 15.5 fusion.46
  705.9 6.8 convert_element_type.110
  712.7 3.2 fusion.16
  715.9 63.8 %all-reduce.14.cloned.1.call-done = f32[1024,2048]{1,0:T(8,128)} async-done(((f32[1024,2048]{1,0:T(8,128)}), f32[1024,2048]{1,0:T(8,128)}) %all-reduce.14.cloned.1.call-update) | async-done | bytes 8388624 | tf_op jit(solution)/shard_map/psum | solution.py:212
  779.7 8.2 fusion.7
  787.9 38.8 %all-reduce.2 = (f32[2048]{0:T(1024)S(1)}, f32[2048]{0:T(1024)S(1)}) all-reduce(f32[2048]{0:T(1024)S(1)} %get-tuple-element.13, f32[2048]{0:T(1024)S(1)} %copy-done.34), channel_id=2, replica_groups=mesh['dp'=8,'tensor'=4] {'dp'}, use_global_device_ids=true, to_apply=%region_13.14.clone | all-reduce | flops 4096 | bytes 32768
  828.0 4.4 fusion.13
  832.4 41.1 %reduce-scatter.14.cloned.1.call-done = f32[512,256]{1,0:T(8,128)} async-done(((f32[512,2048]{1,0:T(8,128)}), f32[512,256]{1,0:T(8,128)}) %reduce-scatter.14.cloned.1.call-update) | async-done | bytes 524304 | tf_op jit(solution)/shard_map/reduce_scatter | solution.py:219
  873.5 91.9 %reduce-scatter.12.cloned.1.call-done = f32[256,512]{1,0:T(8,128)} async-done(((f32[2048,512]{1,0:T(8,128)}), f32[256,512]{1,0:T(8,128)}) %reduce-scatter.12.cloned.1.call-update) | async-done | bytes 524304 | tf_op jit(solution)/shard_map/reduce_scatter | solution.py:218
  965.4 92.4 %reduce-scatter.10.cloned.1.call-done = f32[256,512]{1,0:T(8,128)} async-done(((f32[2048,512]{1,0:T(8,128)}), f32[256,512]{1,0:T(8,128)}) %reduce-scatter.10.cloned.1.call-update) | async-done | bytes 524304 | tf_op jit(solution)/shard_map/reduce_scatter | solution.py:217
  1057.7 91.8 %reduce-scatter.8.cloned.1.call-done = f32[256,512]{1,0:T(8,128)} async-done(((f32[2048,512]{1,0:T(8,128)}), f32[256,512]{1,0:T(8,128)}) %reduce-scatter.8.cloned.1.call-update) | async-done | bytes 524304 | tf_op jit(solution)/shard_map/reduce_scatter | solution.py:216
  1149.5 287.3 %reduce-scatter.20.cloned.1.call-done = f32[2048,256]{1,0:T(8,128)} async-done(((f32[2048,2048]{1,0:T(8,128)}), f32[2048,256]{1,0:T(8,128)}) %reduce-scatter.20.cloned.1.call-update) | async-done | bytes 2097168 | tf_op jit(solution)/shard_map/reduce_scatter | solution.py:222
  1436.8 286.0 %reduce-scatter.18.cloned.1.call-done = f32[256,2048]{1,0:T(8,128)} async-done(((f32[2048,2048]{1,0:T(8,128)}), f32[256,2048]{1,0:T(8,128)}) %reduce-scatter.18.cloned.1.call-update) | async-done | bytes 2097168 | tf_op jit(solution)/shard_map/reduce_scatter | solution.py:221
  1722.8 286.6 %reduce-scatter.16.cloned.1.call-done = f32[256,2048]{1,0:T(8,128)} async-done(((f32[2048,2048]{1,0:T(8,128)}), f32[256,2048]{1,0:T(8,128)}) %reduce-scatter.16.cloned.1.call-update) | async-done | bytes 2097168 | tf_op jit(solution)/shard_map/reduce_scatter | solution.py:220
  (143 shorter events, 21.6 us)
Async XLA Ops:
  7.2 101.8 %copy-start = (bf16[512,2048]{1,0:T(8,128)(2,1)S(1)}, bf16[512,2048]{1,0:T(8,128)(2,1)}, u32[]{:S(2)}) copy-start(bf16[512,2048]{1,0:T(8,128)(2,1)} %param.18) | copy-start | bytes 6291460
  7.2 39.6 %all-gather.3.cloned.1.call-start = ((), (), s32[]{:S(2)}) async-start(), calls=%async_computation.7 | async-start | bytes 5242880 | tf_op jit(solution)/shard_map/all_gather | solution.py:107
  7.9 259.8 %all-reduce.8.cloned.1.call-start = ((), (), s32[]{:S(2)}) async-start(), calls=%async_computation.8 | async-start | bytes 16777216 | tf_op jit(solution)/shard_map/psum | solution.py:146
  8.7 81.6 %copy-start.32 = (f32[2048]{0:T(1024)}, f32[2048]{0:T(1024)S(1)}, u32[]{:S(2)}) copy-start(f32[2048]{0:T(1024)S(1)} %convert_element_type.113) | copy-start | bytes 24580
  11.6 47.0 %copy-start.18 = (f32[1024,32]{0,1:T(8,128)}, f32[1024,32]{0,1:T(8,128)S(1)}, u32[]{:S(2)}) copy-start(f32[1024,32]{0,1:T(8,128)S(1)} %get-tuple-element.35) | copy-start | bytes 393220
  11.6 47.0 %copy-start.20 = (f32[1024,32]{0,1:T(8,128)}, f32[1024,32]{0,1:T(8,128)S(1)}, u32[]{:S(2)}) copy-start(f32[1024,32]{0,1:T(8,128)S(1)} %get-tuple-element.36) | copy-start | bytes 393220
  13.6 79.2 %copy-start.5 = (pred[1024,1024]{0,1:T(8,128)(4,1)}, pred[1024,1024]{0,1:T(8,128)(4,1)S(1)}, u32[]{:S(2)}) copy-start(pred[1024,1024]{0,1:T(8,128)(4,1)S(1)} %fusion.12) | copy-start | bytes 3145732
  50.5 39.8 %copy-start.30 = (f32[1024]{0:T(1024)}, f32[1024]{0:T(1024)S(1)}, u32[]{:S(2)}) copy-start(f32[1024]{0:T(1024)S(1)} %get-tuple-element.38) | copy-start | bytes 12292
  50.5 5.5 copy-start.3
  50.5 5.5 copy-start.39
  60.2 15.1 copy-start.12
  60.2 15.1 copy-start.14
  75.4 14.9 copy-start.10
  92.8 15.3 copy-start.22
  109.0 6.5 copy-start.36
  109.0 6.5 copy-start.37
  114.7 189.6 %all-gather.5.cloned.1.call-start = ((), (), s32[]{:S(2)}) async-start(), calls=%async_computation.10 | async-start | bytes 5242880 | tf_op jit(solution)/shard_map/all_gather | solution.py:108
  115.4 390.4 %all-reduce.12.cloned.1.call-start = ((), (), s32[]{:S(2)}) async-start(), calls=%async_computation.11 | async-start | bytes 16777216 | tf_op jit(solution)/shard_map/psum | solution.py:168
  273.5 17.5 copy-start.2
  274.3 16.7 copy-start.8
  326.3 12.7 copy-start.44
  352.8 360.0 %all-reduce.10.cloned.1.call-start = ((), (), s32[]{:S(2)}) async-start(), calls=%async_computation.9 | async-start | bytes 8388608 | tf_op jit(solution)/shard_map/psum | solution.py:156
  366.7 413.0 %all-reduce.14.cloned.1.call-start = ((), (), s32[]{:S(2)}) async-start(), calls=%async_computation.12 | async-start | bytes 16777216 | tf_op jit(solution)/shard_map/psum | solution.py:212
  505.8 8.7 copy-start.4
  505.9 10.2 copy-start.9
  520.7 3.7 copy-start.7
  520.7 3.7 copy-start.6
  524.5 16.4 copy-start.23
  524.5 16.4 copy-start.24
  593.8 11.4 copy-start.13
  593.8 11.4 copy-start.15
  605.2 8.9 copy-start.19
  605.2 8.9 copy-start.21
  615.0 5.8 copy-start.28
  626.9 9.1 copy-start.31
  626.9 9.1 copy-start.33
  626.9 246.6 %reduce-scatter.14.cloned.1.call-start = ((), (), s32[]{:S(2)}) async-start(), calls=%async_computation.16 | async-start | bytes 4718592 | tf_op jit(solution)/shard_map/reduce_scatter | solution.py:219
  635.9 7.1 copy-start.29
  635.9 329.4 %reduce-scatter.12.cloned.1.call-start = ((), (), s32[]{:S(2)}) async-start(), calls=%async_computation.15 | async-start | bytes 4718592 | tf_op jit(solution)/shard_map/reduce_scatter | solution.py:218
  643.0 7.3 copy-start.27
  643.0 414.8 %reduce-scatter.10.cloned.1.call-start = ((), (), s32[]{:S(2)}) async-start(), calls=%async_computation.14 | async-start | bytes 4718592 | tf_op jit(solution)/shard_map/reduce_scatter | solution.py:217
  650.2 499.3 %reduce-scatter.8.cloned.1.call-start = ((), (), s32[]{:S(2)}) async-start(), calls=%async_computation.13 | async-start | bytes 4718592 | tf_op jit(solution)/shard_map/reduce_scatter | solution.py:216
  657.1 779.6 %reduce-scatter.20.cloned.1.call-start = ((), (), s32[]{:S(2)}) async-start(), calls=%async_computation.19 | async-start | bytes 18874368 | tf_op jit(solution)/shard_map/reduce_scatter | solution.py:222
  673.1 1049.7 %reduce-scatter.18.cloned.1.call-start = ((), (), s32[]{:S(2)}) async-start(), calls=%async_computation.18 | async-start | bytes 18874368 | tf_op jit(solution)/shard_map/reduce_scatter | solution.py:221
  688.5 1320.8 %reduce-scatter.16.cloned.1.call-start = ((), (), s32[]{:S(2)}) async-start(), calls=%async_computation.17 | async-start | bytes 18874368 | tf_op jit(solution)/shard_map/reduce_scatter | solution.py:220
  715.9 72.0 %copy-start.34 = (f32[2048]{0:T(1024)S(1)}, f32[2048]{0:T(1024)}, u32[]{:S(2)}) copy-start(f32[2048]{0:T(1024)} %get-tuple-element.11) | copy-start | bytes 24580
  715.9 112.1 %copy-start.35 = (f32[1024]{0:T(1024)S(1)}, f32[1024]{0:T(1024)}, u32[]{:S(2)}) copy-start(f32[1024]{0:T(1024)} %get-tuple-element.37) | copy-start | bytes 12292
  779.7 1229.6 %copy-start.1 = (bf16[512,2048]{1,0:T(8,128)(2,1)S(1)}, bf16[512,2048]{1,0:T(8,128)(2,1)}, u32[]{:S(2)}) copy-start(bf16[512,2048]{1,0:T(8,128)(2,1)} %param.18) | copy-start | bytes 6291460
  (10 other events, 20.5 us)
Sparse Core Ops, SparseCore 0:
  9.6 37.1 all-gather.2
  114.8 152.8 all-reduce.7
  269.3 34.6 all-gather.4
  352.9 152.9 all-reduce.11
  508.1 85.6 all-reduce.9
  627.0 152.6 all-reduce.13
  784.3 89.0 reduce-scatter.13
  877.7 87.6 reduce-scatter.11
  970.0 87.6 reduce-scatter.9
  1061.8 87.6 reduce-scatter.7
  1154.3 282.3 reduce-scatter.19
  1441.0 281.7 reduce-scatter.17
  1727.6 281.6 reduce-scatter.15
where the time goes:
time: 2020 us
  waiting for transfers between devices  1570 us (78%)
  matrix products  289 us (14%)
  other arithmetic  97.5 us (5%)
  blocking collectives  38.8 us (2%)
    reduce_scatter x1, waiting for transfers between devices, shards(): lax.psum_scatter(grad_down, 'dp', scatter_dimension=1, tiled=True)  287 us
    reduce_scatter x1, waiting for transfers between devices, shards(): lax.psum_scatter(grad_gate, 'dp', scatter_dimension=0, tiled=True)  287 us
    reduce_scatter x1, waiting for transfers between devices, shards(): lax.psum_scatter(grad_up, 'dp', scatter_dimension=0, tiled=True)  286 us
    psum x1, waiting for transfers between devices, shards(): lax.psum(jnp.dot(attended, w_out, preferred_element_type=jnp.float32), 't...  152 us
    psum x1, waiting for transfers between devices, shards(): lax.psum(times_transposed(d_gate, w_gate) + times_transposed(d_up, w_up),...  139 us
    reduce_scatter x1, waiting for transfers between devices, shards(): lax.psum_scatter(grad_key, 'dp', scatter_dimension=0, tiled=True)  92.4 us
    reduce_scatter x1, waiting for transfers between devices, shards(): lax.psum_scatter(grad_value, 'dp', scatter_dimension=0, tiled=True)  91.9 us
    reduce_scatter x1, waiting for transfers between devices, shards(): lax.psum_scatter(grad_query, 'dp', scatter_dimension=0, tiled=True)  91.8 us
  transfers between devices with their start and end apart: 13, of which 11 were waited for; matrix products, arithmetic and copies ran while one was open for 14% of the time, Pallas kernels for 0%

commit v1 on v0

v1 whole, which is shorter than its diff:
```python
import functools
import math

import jax
import jax.numpy as jnp
from jax import lax
from jax.experimental import pallas as pl
from jax.experimental.pallas import tpu as pltpu
from jax.sharding import PartitionSpec as P

HD = 64
TILE = 128
BF = jnp.bfloat16
F32 = jnp.float32
CORE_PERM = [(0, 1), (1, 0), (2, 3), (3, 2)]
Y_PERM = [(0, 2), (2, 0), (1, 3), (3, 1)]
DIAG_PERM = [(0, 3), (3, 0), (1, 2), (2, 1)]
MIB = 1024 * 1024
T, C, Y, X, Z = range(5)


def dot(a, b):
    return lax.dot_general(a, b, (((1,), (0,)), ((), ())), preferred_element_type=F32)


def dot_rows(a, b):
    return lax.dot_general(a, b, (((0,), (0,)), ((), ())), preferred_element_type=F32)


def dot_t(a, b):
    return lax.dot_general(a, b, (((1,), (1,)), ((), ())), preferred_element_type=F32)


def core_go(a):
    return lax.ppermute(a, "tensor", CORE_PERM)


def y_go(a):
    return lax.ppermute(a, "tensor", Y_PERM)


def diag_go(a):
    return lax.ppermute(a, "tensor", DIAG_PERM)


def x_go(a):
    return lax.ppermute(a, "dp", [(i, i ^ 1) for i in range(lax.axis_size("dp"))])


def sds(shape, dtype=BF):
    return jax.ShapeDtypeStruct(shape, dtype)


def call(name, us, body, scal, grid, ins, outs, deps=(), scratch=(), aliases=None, limit=24, mark=False):
    n_in, n_dep, n_out = len(ins), len(deps), len(outs)
    if mark:
        outs = list(outs) + [(sds((8, 128), F32), (8, 128), fixed(0, 0))]

    def wrapped(s, *refs):
        if mark:
            refs[n_in + n_dep + n_out][...] = jnp.zeros((8, 128), F32)
            refs = refs[: n_in + n_dep + n_out] + refs[n_in + n_dep + n_out + 1 :]
        body(s, *refs[:n_in], *refs[n_in + n_dep :])

    spec = lambda block, index: pl.BlockSpec(memory_space=pl.ANY) if block is None else pl.BlockSpec(block, index)
    got = pl.pallas_call(
        wrapped,
        grid_spec=pltpu.PrefetchScalarGridSpec(
            num_scalar_prefetch=1,
            grid=grid,
            in_specs=[spec(b, i) for _, b, i in ins] + [pl.BlockSpec(memory_space=pl.ANY)] * n_dep,
            out_specs=[spec(b, i) for _, b, i in outs],
            scratch_shapes=list(scratch),
        ),
        out_shape=[o for o, _, _ in outs],
        input_output_aliases={k + 1: v for k, v in (aliases or {}).items()},
        compiler_params=pltpu.CompilerParams(vmem_limit_bytes=limit * MIB),
        cost_estimate=pl.CostEstimate(flops=int(us * 1.1e9), bytes_accessed=int(us * 3.6e6), transcendentals=0),
        name=name,
    )(scal, *[a for a, _, _ in ins], *deps)
    return got[0] if len(outs) == 1 else got


def fixed(*at):
    return lambda *_: at


def quarter_of(s, k):
    return 2 * lax.bitwise_xor(s[C], k % 2) + lax.bitwise_xor(s[Y], k // 2)


def swap_halves(v):
    width = v.shape[1]
    lane = lax.broadcasted_iota(jnp.int32, v.shape, 1) % HD
    return jnp.where(lane < HD // 2, pltpu.roll(v, width - HD // 2, 1), pltpu.roll(v, HD // 2, 1))


def widen(tab, width):
    return jnp.concatenate([tab] * (width // tab.shape[1]), axis=1)


def qkv_body(s, h0, h1, h2, h3, gain, wq, wk, wv, cos, sin, x_out, n_out, out):
    part = h0.shape[1]
    for k, h in enumerate((h0, h1, h2, h3)):
        at = pl.multiple_of(lax.bitwise_xor(s[T], k) * part, part)
        x_out[:, pl.ds(at, part)] = h[...]
    vals = x_out[...].astype(F32)
    inv = lax.rsqrt(jnp.mean(vals * vals, axis=1, keepdims=True) + 1e-05)
    n = (vals * inv * gain[...].astype(F32)).astype(BF)
    n_out[...] = n
    width = wq.shape[1]
    c, sn = widen(cos[...], 256), widen(sin[...], 256)
    for m, w in enumerate((wq, wk)):
        for at in range(0, width, 256):
            z = dot(n, w[:, at : at + 256])
            out[:, m * width + at : m * width + at + 256] = (z * c + swap_halves(z) * sn).astype(BF)
    for at in range(0, width, 256):
        out[:, 2 * width + at : 2 * width + at + 256] = dot(n, wv[:, at : at + 256]).astype(BF)


def qkv(scal, pieces, gain, wq, wk, wv, cos, sin, deps):
    slots, part = pieces[0].shape
    full, width = wq.shape
    blk = 256
    row = lambda i, s: (i, 0)
    return call(
        "qkv",
        14,
        qkv_body,
        scal,
        (slots // blk,),
        [(p, (blk, part), row) for p in pieces]
        + [(gain, (1, full), fixed(0, 0))]
        + [(w, (full, width), fixed(0, 0)) for w in (wq, wk, wv)]
        + [(cos, (blk, 128), row), (sin, (blk, 128), row)],
        [
            (sds((slots, full)), (blk, full), row),
            (sds((slots, full)), (blk, full), row),
            (sds((slots, 3 * width)), (blk, 3 * width), row),
        ],
        deps,
        limit=36,
    )


def mask_bias(seq_col, key_row, first, count):
    parts = []
    rows = seq_col[first : first + count, :]
    if first:
        parts.append(jnp.where(rows == key_row[:, :first], 0.0, -1e9))
    r = lax.broadcasted_iota(jnp.int32, (count, count), 0)
    c = lax.broadcasted_iota(jnp.int32, (count, count), 1)
    same = rows == key_row[:, first : first + count]
    parts.append(jnp.where((same & (c < r)) | (c == r), 0.0, -1e9))
    return parts[0] if len(parts) == 1 else jnp.concatenate(parts, axis=1)


def head_only(v, lane, h):
    return jnp.where(lane if h == 0 else jnp.logical_not(lane), v, jnp.zeros_like(v))


def attn_body(s, q_ref, k_ref, v_ref, seq_ref, key_ref, o_ref, lse_ref, *, blk):
    slots = q_ref.shape[0]
    lane = lax.broadcasted_iota(jnp.int32, (blk, 128), 1) < HD
    for i in range(slots // blk):
        first, n = i * blk, (i + 1) * blk
        bias = mask_bias(seq_ref, key_ref, first, blk)
        q2 = q_ref[first:n, :] * jnp.asarray(0.125, BF)
        k2 = k_ref[:n, :]
        v2 = v_ref[:n, :]
        outs, lses = [], []
        for h in range(2):
            sc = dot_t(head_only(q2, lane, h), k2) + bias
            top = jnp.max(sc, axis=1, keepdims=True)
            e = jnp.exp(sc - top)
            total = jnp.sum(e, axis=1, keepdims=True)
            outs.append(dot(e.astype(BF), v2) * (1.0 / total))
            lses.append(top + jnp.log(total))
        o_ref[first:n, :] = jnp.where(lane, outs[0], outs[1]).astype(BF)
        lse_ref[first:n, :] = jnp.where(lane, lses[0], lses[1])


def attention(scal, qkv_all, seq_col, key_row, deps):
    slots, width = qkv_all.shape
    width //= 3
    pairs = width // 128
    third = lambda m: lambda i, s: (0, m * pairs + i)
    return call(
        "attention",
        17,
        functools.partial(attn_body, blk=256),
        scal,
        (pairs,),
        [(qkv_all, (slots, 128), third(m)) for m in range(3)]
        + [(seq_col, (slots, 1), fixed(0, 0)), (key_row, (1, slots), fixed(0, 0))],
        [(sds((slots, width), d), (slots, 128), third(0)) for d in (BF, F32)],
        deps,
        limit=24,
    )


def attn_back_body(
    s, q_ref, k_ref, v_ref, o_ref, do_ref, lse_ref, seq_ref, key_ref, cos, sin, dq_ref, dk_ref, dv_ref, dk_acc, dv_acc, *, blk
):
    slots = q_ref.shape[0]
    lane = lax.broadcasted_iota(jnp.int32, (blk, 128), 1) < HD
    dk_acc[...] = jnp.zeros_like(dk_acc)
    dv_acc[...] = jnp.zeros_like(dv_acc)
    for i in range(slots // blk):
        first, n = i * blk, (i + 1) * blk
        bias = mask_bias(seq_ref, key_ref, first, blk)
        q2 = q_ref[first:n, :] * jnp.asarray(0.125, BF)
        do2 = do_ref[first:n, :]
        lse2 = lse_ref[first:n, :]
        prod = do2.astype(F32) * o_ref[first:n, :].astype(F32)
        k2 = k_ref[:n, :]
        v2 = v_ref[:n, :]
        dqs = []
        for h in range(2):
            qm = head_only(q2, lane, h)
            dom = head_only(do2, lane, h)
            delta = jnp.sum(head_only(prod, lane, h), axis=1, keepdims=True)
            p = jnp.exp(dot_t(qm, k2) + bias - lse2[:, h * HD : h * HD + 1])
            ds = (p * (dot_t(dom, v2) - delta)).astype(BF)
            dv_acc[:n, :] += dot_rows(p.astype(BF), dom)
            dk_acc[:n, :] += dot_rows(ds, qm)
            dqs.append(dot(ds, k2))
        dq = jnp.where(lane, dqs[0], dqs[1]) * 0.125
        dq_ref[first:n, :] = (dq * cos[first:n, :] - swap_halves(dq) * sin[first:n, :]).astype(BF)
    dk = dk_acc[...]
    dk_ref[...] = (dk * cos[...] - swap_halves(dk) * sin[...]).astype(BF)
    dv_ref[...] = dv_acc[...].astype(BF)


def attention_back(scal, half, qkv_all, o, do, lse, seq_col, key_row, cos, sin, deps):
    slots, width = o.shape
    pairs = width // 128
    count = pairs // 2
    third = lambda m: lambda i, s: (0, m * pairs + half * count + i)
    return call(
        "attention_back",
        13,
        functools.partial(attn_back_body, blk=256),
        scal,
        (count,),
        [(qkv_all, (slots, 128), third(m)) for m in range(3)]
        + [(a, (slots, 128), third(0)) for a in (o, do, lse)]
        + [(seq_col, (slots, 1), fixed(0, 0)), (key_row, (1, slots), fixed(0, 0))]
        + [(cos, (slots, 128), fixed(0, 0)), (sin, (slots, 128), fixed(0, 0))],
        [(sds((slots, width // 2)), (slots, 128), lambda i, s: (0, i))] * 3,
        deps,
        scratch=[pltpu.VMEM((slots, 128), F32)] * 2,
        limit=56,
    )


def tensor_body(s, *refs, n_pairs, op, mode):
    acc = None
    for p in range(n_pairs):
        term = op(refs[p][...], refs[n_pairs + p][...])
        acc = term if acc is None else acc + term
    rest = refs[2 * n_pairs :]
    if mode == "send":
        far, near = rest
        half = acc.shape[0] // 2
        low, high = acc[:half], acc[half:]
        far[...] = jnp.where(s[Y] == 0, high, low).astype(BF)
        near[...] = jnp.where(s[Y] == 0, low, high).astype(BF)
    else:
        got, out = rest
        out[...] = (acc + got[...].astype(F32)).astype(out.dtype)


def tensor_part(scal, mode, pairs, op, got, deps):
    slots = pairs[0][0].shape[0]
    quarter = slots // 4
    full = pairs[0][1].shape[1 if op is dot else 0]
    side = lambda at: lambda j, s: (j, at)
    tile = 512
    n_rows = 2 * quarter if mode == "send" else quarter
    row = {
        "send": lambda j, s: (1 - s[C], 0),
        "far": lambda j, s: (2 * s[C] + 1 - s[Y], 0),
        "near": lambda j, s: (2 * s[C] + s[Y], 0),
    }[mode]
    ins = [(a, (n_rows, a.shape[1]), row) for a, _, _ in pairs]
    for a, w, at in pairs:
        if op is dot:
            ins.append((w, (w.shape[0], tile), lambda j, s: (0, j)))
        else:
            ins.append((w, (tile, a.shape[1]), side(at)))
    col = lambda j, s: (0, j)
    if mode == "send":
        outs = [(sds((quarter, full)), (quarter, tile), col)] * 2
    else:
        ins.append((got, (quarter, tile), col))
        outs = [(sds((quarter, full), BF if mode == "far" else F32), (quarter, tile), col)]
    body = functools.partial(tensor_body, n_pairs=len(pairs), op=op, mode=mode)
    return call("tensor_" + mode, 5 if len(pairs) == 1 else 7, body, scal, (full // tile,), ins, outs, deps, limit=56)


def row_mean(v):
    return jnp.mean(v, axis=1, keepdims=True)


def own_quarter(g, s):
    return (quarter_of(s, 0), 0)


def back_of_norm(values, gain, upstream):
    inv = lax.rsqrt(row_mean(values * values) + 1e-05)
    gained = upstream * gain
    grad = jnp.sum(upstream * values * inv, axis=0, keepdims=True)
    return inv * gained - values * (inv * inv * inv) * row_mean(gained * values), grad


def joined(b0, from_x, from_y):
    return b0[...] + from_x[...].astype(F32) + from_y[...].astype(F32)


def norm2_back_body(s, b0, from_x, from_y, hres, live, gain, dm, da_out, back_out, grad_out):
    back, grad = back_of_norm(hres[...], gain[...].astype(F32), joined(b0, from_x, from_y))
    back_out[...] = back
    grad_out[...] = grad
    da_out[...] = (dm[...].astype(F32) + live[...] * back).astype(BF)


def norm2_back(scal, parts, hres, live, gain, dm, deps):
    rows, full = hres.shape
    whole = ((rows, full), fixed(0, 0))
    return call(
        "norm2_back", 7, norm2_back_body, scal, (1,),
        [(p, *whole) for p in parts]
        + [(hres, *whole), (live, (rows, 1), own_quarter), (gain, (1, full), fixed(0, 0)), (dm, *whole)],
        [(sds((rows, full)), *whole), (sds((rows, full), F32), *whole), (sds((1, full), F32), (1, full), fixed(0, 0))],
        deps,
    )


def feature_pieces(s, value, outs, hold):
    part = outs[0].shape[1]
    hold[...] = value.astype(BF)
    for k, out in enumerate(outs):
        out[...] = hold[:, pl.ds(pl.multiple_of(lax.bitwise_xor(s[T], k) * part, part), part)]


def norm1_back_body(s, near, back, x_own, gain, back_two, o0, o1, o2, o3, grad_out, hold):
    value, grad = back_of_norm(x_own[...].astype(F32), gain[...].astype(F32), near[...] + back[...].astype(F32))
    grad_out[...] = grad
    feature_pieces(s, value + back_two[...], (o0, o1, o2, o3), hold)


def norm1_back(scal, near, back, x_full, gain, back_two, deps):
    rows, full = near.shape
    whole = ((rows, full), fixed(0, 0))
    piece = (sds((rows, full // 4)), (rows, full // 4), fixed(0, 0))
    return call(
        "norm1_back", 6, norm1_back_body, scal, (1,),
        [(near, *whole), (back, *whole), (x_full, (rows, full), own_quarter), (gain, (1, full), fixed(0, 0)),
         (back_two, *whole)],
        [piece] * 4 + [(sds((1, full), F32), (1, full), fixed(0, 0))],
        deps,
        scratch=[pltpu.VMEM((rows, full), BF)],
        limit=56,
    )


def layer_body(s, b0, from_x, from_y, hres, live, o0, o1, o2, o3, hold):
    value = hres[...] + live[...] * joined(b0, from_x, from_y)
    feature_pieces(s, value, (o0, o1, o2, o3), hold)


def layer_rows(scal, parts, hres, live, deps):
    rows, full = hres.shape
    whole = ((rows, full), fixed(0, 0))
    piece = (sds((rows, full // 4)), (rows, full // 4), fixed(0, 0))
    return call(
        "layer_rows", 5, layer_body, scal, (1,),
        [(p, *whole) for p in parts]
        + [(hres, *whole), (live, (rows, 1), own_quarter)],
        [piece] * 4,
        deps,
        scratch=[pltpu.VMEM((rows, full), BF)],
    )


def place_body(s, *refs):
    out = refs[-1]
    rows = refs[0].shape[0]
    for k in range(4):
        at = pl.multiple_of(quarter_of(s, k) * rows, rows)
        value = refs[k][...]
        if len(refs) == 6:
            value = (value.astype(F32) + refs[4][pl.ds(at, rows), :].astype(F32)).astype(BF)
        out[pl.ds(at, rows), :] = value


def place_rows(scal, pieces, extra, deps):
    rows, cols = pieces[0].shape
    ins = [(p, (rows, cols), fixed(0, 0)) for p in pieces]
    if extra is not None:
        ins.append((extra, (4 * rows, cols), fixed(0, 0)))
    return call("place", 4, place_body, scal, (1,), ins, [(sds((4 * rows, cols)), (4 * rows, cols), fixed(0, 0))], deps)


def to_features(pieces):
    return [pieces[0], core_go(pieces[1]), y_go(pieces[2]), diag_go(pieces[3])]


def places():
    d, t = lax.axis_index("dp"), lax.axis_index("tensor")
    x, c, y = d % 2, t % 2, t // 2
    return x, c, y, {"tensor": t + 1 - 2 * c}, {"tensor": t + 2 - 4 * y}, {"dp": d + 1 - 2 * x}


def greet(*others):
    barrier = pltpu.get_barrier_semaphore()
    for other in others:
        pl.semaphore_signal(barrier, inc=1, device_id=other, device_id_type=pl.DeviceIdType.MESH)
    pl.semaphore_wait(barrier, len(others))


def remote(src, dst, send_sem, recv_sem, k, other):
    return pltpu.make_async_remote_copy(
        src_ref=src,
        dst_ref=dst,
        send_sem=send_sem.at[k],
        recv_sem=recv_sem.at[k],
        device_id=other,
        device_id_type=pl.DeviceIdType.MESH,
    )


def front_body(
    att, w_out, x_full, live, gain, dm0, dm0c, dmy, dmx, dmxc, wg, wu, wd,
    n2_out, hid_out, dga_out, dua_out, dm_out, down_out, hres_out,
    att_v, wo_v, xo_v, wg_v, wu_v, wd_v, n2_v, dm_v, snd, rcv, far_v, near_v, y_in, dyc, dxy, dxyc, hid_v, stage, sums,
    local, pieces_in, out_sem, whole_sem, sum_sem, send_sem, recv_sem,
):
    x, c, y, core, across_y, across_x = places()
    t = 2 * y + c
    rows, units, part = n2_v.shape[1], wg_v.shape[1], dmy.shape[1]

    def at(qc, qy):
        return pl.ds(pl.multiple_of((2 * qc + qy) * rows, rows), rows)

    def features(kc, ky):
        of = t + kc * (1 - 2 * c) + ky * (2 - 4 * y)
        return pl.ds(pl.multiple_of(of * part, part), part)

    dm_core = remote(dmy, dyc, send_sem, recv_sem, 3, core)
    dm_diag = remote(dmy, dxy, send_sem, recv_sem, 4, across_x)
    dm_on = remote(dxy, dxyc, send_sem, recv_sem, 5, core)
    half = pl.ds(pl.multiple_of(x * units, units), units)
    first = [
        pltpu.make_async_copy(att, att_v, local.at[0]),
        pltpu.make_async_copy(w_out, wo_v, local.at[1]),
        pltpu.make_async_copy(x_full.at[at(c, y), :], xo_v, local.at[2]),
    ]
    weights = [
        pltpu.make_async_copy(wg.at[:, half], wg_v, local.at[3]),
        pltpu.make_async_copy(wu.at[:, half], wu_v, local.at[4]),
        pltpu.make_async_copy(wd.at[half, :], wd_v, local.at[5]),
    ]
    for load in first:
        load.start()
    greet(core, across_y, across_x)
    dm_core.start()
    dm_diag.start()
    for load in weights:
        load.start()
    own_dm, pair_dm = [], []
    for r in range(8):
        ky, kx, kc = (r // 2) % 2, r // 4, r % 2
        from_rows = at(c + kc * (1 - 2 * c), y + ky * (1 - 2 * y))
        sources = ((dmx, 0, 0), (dmxc, 1, 0)) if kx else ((dm0, 0, 0), (dm0c, 1, 0), (dmy, 0, 1))
        for n, (source, fc, fy) in enumerate(sources):
            copy = pltpu.make_async_copy(
                source.at[from_rows, :], dm_v.at[r, :, features(fc, fy)], pieces_in.at[3 * r + n]
            )
            copy.start()
            (pair_dm if kx else own_dm).append(copy)

    for load in first:
        load.wait()

    def product(qc, qy, emit):
        left = att_v[at(qc, qy), :]
        for n in range(0, wo_v.shape[1], 256):
            emit(slice(n, n + 256), dot(left, wo_v[:, n : n + 256]))

    to_core = [remote(snd.at[k], rcv.at[k], send_sem, recv_sem, k, core) for k in range(2)]
    to_y = remote(far_v, y_in, send_sem, recv_sem, 2, across_y)
    for k, qy in enumerate((1 - y, y)):

        def put(cols, acc, k=k):
            snd[k, :, cols] = acc.astype(BF)

        product(1 - c, qy, put)
        to_core[k].start()
    to_core[0].wait_recv()

    def put_far(cols, acc):
        far_v[:, cols] = (acc + rcv[0, :, cols].astype(F32)).astype(BF)

    product(c, 1 - y, put_far)
    to_y.start()
    to_core[1].wait_recv()

    def put_near(cols, acc):
        near_v[:, cols] = acc + rcv[1, :, cols].astype(F32)

    product(c, y, put_near)
    for copy in own_dm:
        copy.wait()
    dm_core.wait_recv()
    for r in range(4):
        dm_v[r, :, features(1, 1)] = dyc[at(c + (r % 2) * (1 - 2 * c), y + (r // 2) * (1 - 2 * y)), :]

    to_y.wait_recv()
    hres = xo_v[...].astype(F32) + live[at(c, y), :] * (near_v[...] + y_in[...].astype(F32))
    hres_out[...] = hres
    n2_v[0] = (hres * lax.rsqrt(row_mean(hres * hres) + 1e-05) * gain[...].astype(F32)).astype(BF)

    def block_to(r_from, r_to, other):
        return remote(n2_v.at[r_from], n2_v.at[r_to], send_sem, recv_sem, 5 + r_to, other)

    n_y, n_x, n_c = block_to(0, 2, across_y), block_to(0, 4, across_x), block_to(0, 1, core)
    n_c.start()

    @pl.when(c == 0)
    def _():
        n_x.start()

    @pl.when(c == 1)
    def _():
        n_y.start()

    dm_diag.wait_recv()
    dm_on.start()
    for load in weights:
        load.wait()

    outs = (dga_out, dua_out)

    def order(i):
        inner = ((i + 2) // 4) % 2
        return i * (1 - inner) + inner * (2 + (2 * (1 - c) - i + 10) % 4)

    def store(i, k):
        place = pl.ds(pl.multiple_of(order(i) * rows, rows), rows)
        return pltpu.make_async_copy(stage.at[i % 2, k], outs[k].at[place, :], out_sem.at[i, k])

    def store_whole(i, source, out, k):
        place = pl.ds(pl.multiple_of(order(i) * rows, rows), rows)
        return pltpu.make_async_copy(source.at[order(i)], out.at[place, :], whole_sem.at[i, k])

    @pl.loop(0, 8)
    def _(i):
        r = order(i)

        @pl.when((i == 2) & (c == 0))
        def _():
            n_x.wait_send()
            n_y.start()
            n_x.wait_recv()
            block_to(4, 6, across_y).start()
            block_to(4, 5, core).start()

        @pl.when((i == 2) & (c == 1))
        def _():
            n_y.wait_send()
            n_x.start()
            n_y.wait_recv()
            block_to(2, 6, across_x).start()
            block_to(2, 3, core).start()

        @pl.when(i == 2)
        def _():
            for copy in pair_dm:
                copy.wait()
            dm_on.wait_recv()
            for b in range(4, 8):
                here = at(c + (b % 2) * (1 - 2 * c), y + ((b // 2) % 2) * (1 - 2 * y))
                dm_v[b, :, features(0, 1)] = dxy[here, :]
                dm_v[b, :, features(1, 1)] = dxyc[here, :]

        @pl.when((i == 4) & (c == 0))
        def _():
            n_y.wait_recv()
            block_to(2, 3, core).start()

        @pl.when((i == 4) & (c == 1))
        def _():
            n_x.wait_recv()
            block_to(4, 5, core).start()

        @pl.when((i == 1) | (i == 3) | (i == 5) | (i == 7))
        def _():
            block_to(0, r, core).wait_recv()

        @pl.when(i == 6)
        def _():
            block_to(2, 6, across_x).wait_recv()
            block_to(6, 7, core).start()

        store_whole(i, n2_v, n2_out, 0).start()
        store_whole(i, dm_v, dm_out, 1).start()

        @pl.when(i >= 2)
        def _():
            for k in range(2):
                store(i - 2, k).wait()

        for col in range(0, units, 256):
            cols = slice(col, col + 256)
            n = n2_v[r]
            ga = dot(n, wg_v[:, cols])
            ua = dot(n, wu_v[:, cols])
            dhid = dot_t(dm_v[r], wd_v[cols, :])
            sig = jax.nn.sigmoid(ga)
            silu = ga * sig
            hid_v[r, :, cols] = (silu * ua).astype(BF)
            stage[i % 2, 0, :, cols] = (dhid * ua * (sig * (1.0 + ga * (1.0 - sig)))).astype(BF)
            stage[i % 2, 1, :, cols] = (dhid * silu).astype(BF)
        for k in range(2):
            store(i, k).start()
        store_whole(i, hid_v, hid_out, 2).start()

    lines, width = sums.shape[1], sums.shape[3]

    def sum_store(u):
        here = pl.ds(pl.multiple_of(u * 256, 256), 256)
        return pltpu.make_async_copy(sums.at[u % 2], down_out.at[:, here, :], sum_sem.at[u])

    @pl.loop(0, units // 256)
    def _(u):
        @pl.when(u >= 2)
        def _():
            sum_store(u - 2).wait()

        turned = hid_v[:, :, pl.ds(pl.multiple_of(u * 256, 256), 256)].reshape(8 * rows, 256).T
        for n in range(0, lines * width, 256):
            value = dot(turned, dm_v[:, :, n : n + 256].reshape(8 * rows, 256)).astype(BF)
            piece = min(width, 256)
            for m in range(0, 256, piece):
                at_n = (n + m) % width
                sums[u % 2, (n + m) // width, :, at_n : at_n + piece] = value[:, m : m + piece]
        sum_store(u).start()

    for u in range(units // 256 - 2, units // 256):
        sum_store(u).wait()
    for i in (6, 7):
        for k in range(2):
            store(i, k).wait()

    @pl.loop(0, 8)
    def _(i):
        store_whole(i, n2_v, n2_out, 0).wait()
        store_whole(i, dm_v, dm_out, 1).wait()
        store_whole(i, hid_v, hid_out, 2).wait()

    @pl.when(c == 0)
    def _():
        n_y.wait_send()

    @pl.when(c == 1)
    def _():
        n_x.wait_send()

    for copy in (*to_core, to_y, dm_core, dm_diag, dm_on, n_c):
        copy.wait_send()
    for r_from, r_to in ((2, 3), (4, 5), (2, 6), (6, 7)):
        block_to(r_from, r_to, core).wait_send()


def front(att, w_out, x_full, live, gain, dm_pieces, wg, wu, wd, lines):
    slots, width = att.shape
    full = w_out.shape[1]
    rows, units, part = slots // 4, wg.shape[1] // 2, full // 4
    any_spec = pl.BlockSpec(memory_space=pl.ANY)
    vmem = pl.BlockSpec(memory_space=pltpu.VMEM)
    block = lambda *lead: pltpu.VMEM((*lead, rows, full), BF)
    piece = pltpu.VMEM((slots, part), BF)
    return pl.pallas_call(
        front_body,
        in_specs=[any_spec] * 3 + [vmem] * 2 + [any_spec] * 8,
        out_specs=[any_spec] * 6 + [vmem],
        out_shape=[sds((8 * rows, full))] + [sds((8 * rows, units))] * 3
        + [sds((8 * rows, full)), sds((lines, units, full // lines)), sds((rows, full), F32)],
        scratch_shapes=[
            pltpu.VMEM((slots, width), BF),
            pltpu.VMEM((width, full), BF),
            block(),
            pltpu.VMEM((full, units), BF),
            pltpu.VMEM((full, units), BF),
            pltpu.VMEM((units, full), BF),
            block(8),
            block(8),
            block(2),
            block(2),
            block(),
            pltpu.VMEM((rows, full), F32),
            block(),
            piece,
            piece,
            piece,
            pltpu.VMEM((8, rows, units), BF),
            pltpu.VMEM((2, 2, rows, units), BF),
            pltpu.VMEM((2, lines, 256, full // lines), BF),
            pltpu.SemaphoreType.DMA((6,)),
            pltpu.SemaphoreType.DMA((24,)),
            pltpu.SemaphoreType.DMA((8, 2)),
            pltpu.SemaphoreType.DMA((8, 3)),
            pltpu.SemaphoreType.DMA((units // 256,)),
            pltpu.SemaphoreType.DMA((13,)),
            pltpu.SemaphoreType.DMA((13,)),
        ],
        compiler_params=pltpu.CompilerParams(vmem_limit_bytes=62 * MIB, collective_id=2, has_side_effects=True),
        cost_estimate=pl.CostEstimate(flops=int(80 * 1.1e9), bytes_accessed=int(80 * 3.6e6), transcendentals=0),
        name="front",
    )(att, w_out, x_full, live, gain, *dm_pieces, wg, wu, wd)


def dn2_body(
    dga, dua, hid, wg, wu, wd, hres, dm, live, gain, da_out, back_out, grad_out, m_own, m_x, m_y,
    lefts, ws, wd_v, snd, rcv, kept, sb, via, via2, fx, fy, da_own, da_got, local, send_sem, recv_sem, credit,
):
    x, c, y, core, across_y, across_x = places()
    units, rows = wd_v.shape[0], snd.shape[1]
    half = pl.ds(pl.multiple_of(x * units, units), units)
    side = [slice(0, units), slice(units, 2 * units)]
    loads = [pltpu.make_async_copy(w.at[:, half], ws.at[:, side[p]], local.at[p]) for p, w in enumerate((wg, wu))]
    for kc in (1, 0):
        for p, left in enumerate((dga, dua)):
            loads.append(pltpu.make_async_copy(left.at[:, kc], lefts.at[kc, :, :, side[p]], local.at[2 + 2 * kc + p]))
    loads.append(pltpu.make_async_copy(hres, back_out, local.at[6]))
    loads.append(pltpu.make_async_copy(dm.at[pl.ds(0, rows), :], da_own, local.at[7]))
    loads.append(pltpu.make_async_copy(wd.at[half, :], wd_v, local.at[8]))
    hid_loads = [pltpu.make_async_copy(hid.at[:, kc], lefts.at[kc, :, :, side[0]], local.at[9 + kc]) for kc in range(2)]
    for load in loads:
        load.start()
    greet(core, across_y, across_x)
    for load in loads[:4]:
        load.wait()

    def tiles(kc, m, emit):
        for n in range(0, ws.shape[0], 256):
            emit(slice(n, n + 256), dot_t(lefts[kc, m], ws[n : n + 256, :]))

    def mlp_tiles(kc, m, emit):
        for n in range(0, wd_v.shape[1], 256):
            emit(slice(n, n + 256), dot(lefts[kc, m, :, :units], wd_v[:, n : n + 256]))

    def to_core(m, base):
        return remote(snd.at[m], rcv.at[m], send_sem, recv_sem, base + m, core)

    def send(m, make, base):
        def emit(cols, acc):
            snd[m, :, cols] = acc.astype(BF)

        make(1, m, emit)
        to_core(m, base).start()

    def keep(k, make, base):
        to_core(k, base).wait_recv()

        def emit(cols, acc):
            kept[k, :, cols] = acc + rcv[k, :, cols].astype(F32)

        make(0, k, emit)

    def diagonal_copy(dst, k, other):
        return remote(sb.at[0], dst, send_sem, recv_sem, k, other)

    def send_diagonal(dst, k):
        sb[0] = kept[3].astype(BF)

        @pl.when(c == 0)
        def _():
            diagonal_copy(dst, k, across_x).start()

        @pl.when(c == 1)
        def _():
            diagonal_copy(dst, k, across_y).start()

    @pl.loop(0, 4)
    def _(m):
        send(3 - m, tiles, 0)

    for load in loads[4:]:
        load.wait()
    go_x = remote(sb.at[1], fx, send_sem, recv_sem, 5, across_x)
    go_y = remote(sb.at[2], fy, send_sem, recv_sem, 6, across_y)

    @pl.loop(0, 4)
    def _(i):
        keep(3 - i, tiles, 0)

        @pl.when(i == 0)
        def _():
            send_diagonal(via, 4)

        @pl.when((i == 1) & (c == 0))
        def _():
            sb[1] = kept[2].astype(BF)
            go_x.start()

        @pl.when((i == 2) & (c == 1))
        def _():
            sb[2] = kept[1].astype(BF)
            go_y.start()

    pl.semaphore_signal(credit, inc=1, device_id=core, device_id_type=pl.DeviceIdType.MESH)
    for load in hid_loads:
        load.start()
    cf = c.astype(F32)
    diagonal_copy(via, 4, across_x).wait_recv()

    @pl.when(c == 1)
    def _():
        sb[1] = (kept[2] + via[...].astype(F32)).astype(BF)
        go_x.start()

    @pl.when(c == 0)
    def _():
        sb[2] = (kept[1] + via[...].astype(F32)).astype(BF)
        go_y.start()

    @pl.loop(0, 4)
    def _(m):
        to_core(m, 0).wait_send()

    pl.semaphore_wait(credit, 1)
    for load in hid_loads:
        load.wait()

    @pl.loop(0, 4)
    def _(m):
        send(3 - m, mlp_tiles, 10)

    go_x.wait_recv()
    go_y.wait_recv()
    dn2 = kept[0] + fx[...].astype(F32) + fy[...].astype(F32)
    back, grad = back_of_norm(back_out[...], gain[...].astype(F32), dn2)
    back_out[...] = back
    grad_out[...] = grad

    def at(qc, qy):
        return pl.ds(pl.multiple_of((2 * qc + qy) * rows, rows), rows)

    da_own[...] = (da_own[...].astype(F32) + live[at(c, y), :] * back).astype(BF)
    to_y = remote(da_own, da_got.at[1], send_sem, recv_sem, 8, across_y)
    to_c = remote(da_own, da_got.at[0], send_sem, recv_sem, 7, core)
    on = remote(da_got.at[1], da_got.at[2], send_sem, recv_sem, 9, core)
    to_y.start()
    to_c.start()
    da_out[at(c, y), :] = da_own[...]

    diagonal_copy(via, 4, across_x).wait_send()

    @pl.loop(0, 4)
    def _(i):
        keep(3 - i, mlp_tiles, 10)

        @pl.when(i == 0)
        def _():
            send_diagonal(via2, 14)

    for copy in (go_x, go_y):
        copy.wait_send()
    diagonal_copy(via2, 14, across_x).wait_recv()
    sb[1] = (kept[2] + cf * via2[...].astype(F32)).astype(BF)
    sb[2] = (kept[1] + (1.0 - cf) * via2[...].astype(F32)).astype(BF)
    stores = [
        pltpu.make_async_copy(source, out, local.at[11 + k])
        for k, (source, out) in enumerate(((kept.at[0], m_own), (sb.at[1], m_x), (sb.at[2], m_y)))
    ]
    for store in stores:
        store.start()
    to_c.wait_recv()
    da_out[at(1 - c, y), :] = da_got[0]
    to_y.wait_recv()
    on.start()
    da_out[at(c, 1 - y), :] = da_got[1]
    on.wait_recv()
    da_out[at(1 - c, 1 - y), :] = da_got[2]
    for store in stores:
        store.wait()

    @pl.loop(0, 4)
    def _(m):
        to_core(m, 10).wait_send()

    diagonal_copy(via2, 14, across_x).wait_send()
    for copy in (to_y, to_c, on):
        copy.wait_send()


def dn2_sum(dga, dua, hid, wg, wu, wd, hres, dm, live, gain, deps):
    tokens, units = dga.shape
    full = wg.shape[0]
    rows = tokens // 8
    slots = 4 * rows
    n_dep = len(deps)
    any_spec = pl.BlockSpec(memory_space=pl.ANY)
    vmem = pl.BlockSpec(memory_space=pltpu.VMEM)

    def body(*refs):
        dn2_body(*refs[:10], *refs[10 + n_dep :])

    block = lambda *lead: pltpu.VMEM((*lead, rows, full), BF)
    lefts = [v.reshape(4, 2, rows, units) for v in (dga, dua, hid)]
    return pl.pallas_call(
        body,
        in_specs=[any_spec] * 8 + [vmem] * 2 + [any_spec] * n_dep,
        out_specs=[vmem] * 3 + [any_spec] * 3,
        out_shape=[sds((slots, full)), sds((rows, full), F32), sds((1, full), F32), sds((rows, full), F32)]
        + [sds((rows, full))] * 2,
        scratch_shapes=[
            pltpu.VMEM((2, 4, rows, 2 * units), BF),
            pltpu.VMEM((full, 2 * units), BF),
            pltpu.VMEM((units, full), BF),
            block(4),
            block(4),
            pltpu.VMEM((4, rows, full), F32),
            block(3),
            block(),
            block(),
            block(),
            block(),
            block(),
            block(3),
            pltpu.SemaphoreType.DMA((14,)),
            pltpu.SemaphoreType.DMA((15,)),
            pltpu.SemaphoreType.DMA((15,)),
            pltpu.SemaphoreType.REGULAR,
        ],
        compiler_params=pltpu.CompilerParams(vmem_limit_bytes=62 * MIB, collective_id=1, has_side_effects=True),
        cost_estimate=pl.CostEstimate(flops=int(95 * 1.1e9), bytes_accessed=int(95 * 3.6e6), transcendentals=0),
        name="dn2_sum",
    )(*lefts, wg, wu, wd, hres, dm, live, gain, *deps)


def grad_body(s, a, b, *refs):
    out = refs[-1]
    a_t = a[...].T
    for col in range(0, b.shape[1], 256):
        out[0, :, col : col + 256] = dot(a_t, b[:, col : col + 256]).astype(BF)


def grad_by_rows(scal, a, b, lines, slot, slots, into, deps):
    tokens, m = a.shape
    n = b.shape[1]
    tile = min(256, m // lines)
    per = m // lines // tile
    ins = [(a, (tokens, tile), lambda j, s: (0, j)), (b, b.shape, fixed(0, 0))]
    if into is not None:
        ins.append((into, None, None))
    out = (sds((lines, m // lines, slots * n)), (1, tile, n), lambda j, s: (j // per, j % per, slot))
    aliases = None if into is None else {2: 0}
    return call("grad", 14, grad_body, scal, (m // tile,), ins, [out], deps, aliases=aliases, limit=56)


def line_sum(parts):
    n_dp = lax.axis_size("dp")
    groups = [[2 * z + x for z in range(n_dp // 2)] for x in range(2)]
    return lax.psum_scatter(parts, "dp", scatter_dimension=0, axis_index_groups=groups, tiled=False)


def pair_grad_body(s, a, *refs, n_b, keep):
    a_t = a[...].T
    out = refs[-1]
    width = refs[0].shape[1]
    for k in range(n_b):
        for col in range(0, width, 256):
            value = dot(a_t, refs[k][:, col : col + 256])
            at = k * width + col
            if keep:
                value = value + refs[n_b][0, :, at : at + 256].astype(F32)
            out[0, :, at : at + 256] = value.astype(BF)
    if n_b * width < out.shape[2]:
        out[0, :, n_b * width :] = refs[n_b + 1][0]


def pair_grad(scal, a, bs, lines, got, deps, extra=None):
    rows = a.shape[1] // (2 * lines)
    keep = got is not None
    member = (lambda s: s[X]) if keep else (lambda s: 1 - s[X])
    ins = [(a, (a.shape[0], rows), lambda j, s: (0, 2 * j + member(s)))]
    ins += [(b, b.shape, fixed(0, 0)) for b in bs]
    shard = lambda j, s: (j, 0, 0)
    total = bs[0].shape[1] * len(bs)
    for more in (got, extra):
        if more is not None:
            ins.append((more, (1, rows, more.shape[2]), shard))
    if extra is not None:
        total += extra.shape[2]
    outs = [(sds((lines, rows, total)), (1, rows, total), shard)]
    body = functools.partial(pair_grad_body, n_b=len(bs), keep=keep)
    name = "pair_grad_keep" if keep else "pair_grad_send"
    return call(name, 4 + total // 512, body, scal, (lines,), ins, outs, deps, limit=56)


def flip_body(s, total, out):
    out[...] = total[...].astype(F32).T


def flip(scal, total, first, width, deps):
    rows = total.shape[0]
    part = math.gcd(first, width)
    at = first // part
    return call(
        "flip", 3, flip_body, scal, (width // part,), [(total, (rows, part), lambda g, s: (0, at + g))],
        [(sds((width, rows), F32), (part, rows), lambda g, s: (g, 0))], deps,
    )


def halves_body(s, first, last, *outs):
    part = outs[0].shape[1] // 2
    for k, out in enumerate(outs):
        cols = slice(k * part, (k + 1) * part)
        out[:, :part] = first[:, cols].astype(F32)
        out[:, part:] = last[:, cols].astype(F32)


def head_halves(scal, first, last, part, deps):
    rows = first.shape[0]
    out = (sds((rows, 2 * part), F32), (rows, 2 * part), fixed(0, 0))
    return call(
        "head_halves", 3, halves_body, scal, (1,), [(v, v.shape, fixed(0, 0)) for v in (first, last)], [out] * 3, deps
    )


def pick(s, value, axis, other):
    half = value.shape[axis] // 2
    low, high = (value[:half], value[half:]) if axis == 0 else (value[:, :half], value[:, half:])
    return jnp.where(s[X] == (1 if other else 0), low, high)


def pair_send_body(s, total, out, *, axis):
    out[...] = pick(s, total[...], axis, True)


def pair_send(scal, total, axis, deps):
    shape = tuple(n // 2 if k == axis else n for k, n in enumerate(total.shape))
    body = functools.partial(pair_send_body, axis=axis)
    return call("pair_send", 3, body, scal, (1,), [(total, total.shape, fixed(0, 0))], [(sds(shape), shape, fixed(0, 0))], deps)


def hold_body(s, value, out):
    out[...] = value[...]


def hold(scal, value, deps):
    whole = (value.shape, fixed(0, 0))
    return call("hold", 2, hold_body, scal, (1,), [(value, *whole)], [(sds(value.shape), *whole)], deps)


def pair_join_body(s, total, got, *outs, axis):
    mine = pl.program_id(0) == s[X]
    width = got.shape[1] // len(outs)
    own = pick(s, total[...], axis, False)
    for k, out in enumerate(outs):
        cols = slice(k * width, (k + 1) * width)
        out[...] = jnp.where(mine, own[:, cols], got[:, cols]).astype(F32)


def pair_join(scal, total, got, axis, n_out, deps):
    rows, cols = got.shape
    cols //= n_out
    shape = (rows, 2 * cols) if axis == 0 else (2 * rows, cols)
    place = (lambda g, s: (0, g)) if axis == 0 else (lambda g, s: (g, 0))
    body = functools.partial(pair_join_body, axis=axis)
    return call(
        "pair_join", 4, body, scal, (2,),
        [(total, total.shape, fixed(0, 0)), (got, got.shape, fixed(0, 0))],
        [(sds(shape, F32), (rows, cols), place)] * n_out,
        deps,
    )


def gains_body(one, two, out, have, got, send_sem, recv_sem, *, lines):
    x, c, y, core, across_y, across_x = places()
    z = lax.axis_index("dp") // 2
    along = [{"dp": 2 * ((z + s) % lines) + x} for s in range(1, lines)]
    greet(core, across_y, across_x, *along)
    have[0, 0:1, :] = one[...]
    have[0, 1:2, :] = two[...]
    copies = []
    for k, other in enumerate((core, across_y, across_x)):
        copy = remote(have.at[k], got.at[k], send_sem, recv_sem, k, other)
        copy.start()
        copy.wait_recv()
        have[k + 1] = have[k] + got[k]
        copies.append(copy)
    last = [remote(have.at[3], got.at[3 + s], send_sem, recv_sem, 3 + s, other) for s, other in enumerate(along)]
    for copy in last:
        copy.start()
    total = have[3]
    for s, copy in enumerate(last):
        copy.wait_recv()
        total = total + got[3 + s]
    out[...] = total
    for copy in copies + last:
        copy.wait_send()


def gains_sum(one, two, lines, deps):
    full = one.shape[1]
    vmem = pl.BlockSpec(memory_space=pltpu.VMEM)
    n = 2 + lines

    def body(one, two, *refs):
        gains_body(one, two, *refs[len(deps) :], lines=lines)

    return pl.pallas_call(
        body,
        in_specs=[vmem] * 2 + [pl.BlockSpec(memory_space=pl.ANY)] * len(deps),
        out_specs=vmem,
        out_shape=sds((2, full), F32),
        scratch_shapes=[
            pltpu.VMEM((4, 2, full), F32),
            pltpu.VMEM((n, 2, full), F32),
            pltpu.SemaphoreType.DMA((n,)),
            pltpu.SemaphoreType.DMA((n,)),
        ],
        compiler_params=pltpu.CompilerParams(vmem_limit_bytes=24 * MIB, collective_id=3, has_side_effects=True),
        cost_estimate=pl.CostEstimate(flops=int(12 * 1.1e9), bytes_accessed=int(12 * 3.6e6), transcendentals=0),
        name="gains",
    )(one, two, *deps)


def layout(tile_len, tile_offset):
    tiles = tile_len.shape[0]
    within = jnp.arange(TILE, dtype=jnp.int32)[None, :]
    live = within < tile_len[:, None]
    position = (tile_offset[:, None] * TILE + within).astype(F32)
    seq = jnp.cumsum((tile_offset == 0).astype(jnp.int32))
    seq = jnp.broadcast_to(seq[:, None], (tiles, TILE))
    key = jnp.where(live, seq, -1)
    slots = tiles * TILE
    return live.astype(F32).reshape(slots, 1), position.reshape(slots), seq.reshape(slots, 1), key.reshape(1, slots)


def rope_tables(position):
    frequency = jnp.power(130000.0, -2.0 * jnp.arange(HD // 2, dtype=F32) / HD)
    angles = position[:, None] * frequency[None, :]
    c, s = jnp.cos(angles), jnp.sin(angles)
    return jnp.concatenate([c, c, c, c], axis=1), jnp.concatenate([-s, s, -s, s], axis=1)


def gather_tensor(own):
    far = y_go(own)
    return [own, core_go(own), far, core_go(far)]


def shards(
    hidden_in,
    norm1_gain,
    w_query,
    w_key,
    w_value,
    w_out,
    norm2_gain,
    w_gate,
    w_up,
    w_down,
    tile_len,
    tile_offset,
    cotangent,
):
    n_dp = lax.axis_size("dp")
    lines = n_dp // 2
    d, t = lax.axis_index("dp").astype(jnp.int32), lax.axis_index("tensor").astype(jnp.int32)
    zz, xx = d // 2, d % 2
    yy, cc = t // 2, t % 2
    scal = jnp.stack([t, cc, yy, xx, zz])
    full = w_query.shape[0]
    rows_dp = full // n_dp
    gain_one, gain_two = norm1_gain[None, :], norm2_gain[None, :]
    live, position, seq_col, key_row = layout(tile_len, tile_offset)
    cos, sin = rope_tables(position)

    pieces = gather_tensor(hidden_in)
    dm_own = (cotangent.astype(F32) * live).astype(BF)
    dm_x = x_go(dm_own)
    dm_pieces = [dm_own, core_go(dm_own), y_go(dm_own), dm_x, core_go(dm_x)]

    x_full, n1, qkv_all = qkv(scal, pieces, gain_one, w_query, w_key, w_value, cos, sin, ())
    attended, lse = attention(scal, qkv_all, seq_col, key_row, ())
    n2, hid, dga, dua, dm, down_parts, hres = front(
        attended, w_out, x_full, live, gain_two, dm_pieces, w_gate, w_up, w_down, lines
    )

    narrow = rows_dp % 128 == 0
    down_sum = line_sum(down_parts)
    gate_up = grad_by_rows(scal, n2, dga, lines, 0, 2, None, ())
    gate_up = grad_by_rows(scal, n2, dua, lines, 1, 2, gate_up, ())
    ups_sum = line_sum(gate_up)
    da, back_two, grad_two, m_own, m_x, m_y = dn2_sum(
        dga, dua, hid, w_gate, w_up, w_down, hres, dm, live, gain_two, (gate_up,)
    )
    dob = dob_rows(scal, da, w_out, ())
    back_args = (qkv_all, attended, dob, lse, seq_col, key_row, cos, sin)
    if narrow:
        out_sent = pair_grad(scal, da, [attended], lines, None, (dob,))
        out_got = x_go(out_sent)
        back_a = attention_back(scal, 0, *back_args, (out_sent,))
        sent_a = pair_grad(scal, n1, back_a, lines, None, ())
        got_a = x_go(sent_a)
        m_x = hold(scal, m_x, (sent_a,))
        back_b = attention_back(scal, 1, *back_args, (m_x,))
        sent_b = pair_grad(scal, n1, back_b, lines, None, ())
        got_b = x_go(sent_b)
        out_parts = pair_grad(scal, da, [attended], lines, out_got, (sent_b,))
        last = out_parts
    else:
        back_a = attention_back(scal, 0, *back_args, ())
        back_b = attention_back(scal, 1, *back_args, ())
        last = back_b[0]
    if narrow:
        first_parts = pair_grad(scal, n1, back_a, lines, got_a, (last,), out_parts)
        last = first_parts
    layer_parts = layer_rows(scal, (m_own, x_go(m_x), y_go(m_y)), hres, live, (last,))
    layer_pieces = to_features(layer_parts)
    last = layer_parts[0]
    dn1_pairs = [(v, w, k) for k, back in enumerate((back_a, back_b)) for v, w in zip(back, (w_query, w_key, w_value))]
    send_far, send_near = tensor_part(scal, "send", dn1_pairs, dot_t, None, (last,))
    far = tensor_part(scal, "far", dn1_pairs, dot_t, core_go(send_far), ())
    down_send = pair_send(scal, down_sum, 1, (far,))
    ups_send = pair_send(scal, ups_sum, 0, (down_send,))
    layer_out = place_rows(scal, layer_pieces, None, (ups_send,))
    near = tensor_part(scal, "near", dn1_pairs, dot_t, core_go(send_near), (layer_out,))
    last = near
    if narrow:
        last_parts = pair_grad(scal, n1, back_b, lines, got_b, (near,))
        last = last_parts
    else:
        *first, out_parts = wide_pair_grads(xx, [(n1, v) for v in back_a] + [(da, attended)], lines)
        first_parts = jnp.concatenate(first + [out_parts], axis=2)
        last_parts = jnp.concatenate(wide_pair_grads(xx, [(n1, v) for v in back_b], lines), axis=2)
    first_sum, last_sum = line_sum(first_parts), line_sum(last_parts)
    *in_parts, grad_one = norm1_back(scal, near, y_go(far), x_full, gain_one, back_two, (last,))
    in_pieces = to_features(in_parts)
    all_gains = gains_sum(grad_one, grad_two, lines, ())
    gate_grad, up_grad = pair_join(scal, ups_sum, x_go(ups_send), 0, 2, (all_gains,))
    down_grad = pair_join(scal, down_sum, x_go(down_send), 1, 1, (gate_grad,))
    gains = lax.dynamic_slice_in_dim(all_gains, d * rows_dp, rows_dp, 1)
    part = back_a[0].shape[1]
    out_grad = flip(scal, first_sum, 3 * part, 2 * part, (down_grad,))
    input_grad = place_rows(scal, in_pieces, cotangent, (out_grad,))
    query_grad, key_grad, value_grad = head_halves(scal, first_sum, last_sum, part, (input_grad,))
    return (
        layer_out,
        input_grad,
        gains[0],
        query_grad,
        key_grad,
        value_grad,
        out_grad,
        gains[1],
        gate_grad,
        up_grad,
        down_grad,
    )


def dob_body(s, da, w, out):
    out[...] = dot_t(da[...], w[...]).astype(BF)


def dob_rows(scal, da, w_out, deps):
    slots, full = da.shape
    width = w_out.shape[0]
    blk = 512
    return call(
        "dob", 6, dob_body, scal, (slots // blk,),
        [(da, (blk, full), lambda i, s: (i, 0)), (w_out, (width, full), fixed(0, 0))],
        [(sds((slots, width)), (blk, width), lambda i, s: (i, 0))],
        deps,
    )


def wide_pair_grads(xx, pairs, lines):
    sums = []
    for a, b in pairs:
        parts = dot_rows(a, b).astype(BF)
        parts = parts.reshape(lines, 2, parts.shape[0] // (2 * lines), parts.shape[1])
        got = x_go(lax.dynamic_index_in_dim(parts, 1 - xx, 1, keepdims=False))
        keep = lax.dynamic_index_in_dim(parts, xx, 1, keepdims=False)
        sums.append((keep.astype(F32) + got.astype(F32)).astype(BF))
    return sums


def solution(mesh):
    in_specs = (
        P("dp", "tensor"),
        P(),
        P(None, "tensor"),
        P(None, "tensor"),
        P(None, "tensor"),
        P("tensor", None),
        P(),
        P(None, "tensor"),
        P(None, "tensor"),
        P("tensor", None),
        P("dp"),
        P("dp"),
        P("dp", "tensor"),
    )
    out_specs = (
        P("dp", "tensor"),
        P("dp", "tensor"),
        P("dp"),
        P("dp", "tensor"),
        P("dp", "tensor"),
        P("dp", "tensor"),
        P("tensor", "dp"),
        P("dp"),
        P("dp", "tensor"),
        P("dp", "tensor"),
        P("tensor", "dp"),
    )
    return jax.shard_map(shards, mesh=mesh, in_specs=in_specs, out_specs=out_specs, check_vma=False)
```

time: 2020 us -> 509 us (0.25)
  waiting for transfers between devices: 1570 us -> 45.9 us
  Pallas kernels: 0 us -> 387 us
  matrix products: 289 us -> 0 us
  other arithmetic: 97.5 us -> 6.48 us
  blocking collectives: 38.8 us -> 0 us
  local copies, waits for them, and re-layouts: 7.72 us -> 33.3 us
    reduce_scatter x7 -> x4, waiting for transfers between devices: 1180 us -> 0.02 us  [line_sum(): lax.psum_scatter(parts, 'dp', scatter_dimension=0, axis_index_groups=grou...]
    pallas_call x0 -> x30, Pallas kernels: none -> 387 us  [the longest x27 174 us: call(): pl.pallas_call(wrapped, grid_spec=pltpu.PrefetchScalarGridSpec(num_scalar...]
    psum x4 -> x0, waiting for transfers between devices: 355 us -> none  [the longest x1 152 us: shards(): lax.psum(jnp.dot(attended, w_out, preferred_element_type=jnp.float32), 't...]
    dot_general x27 -> x0, matrix products: 289 us -> none  [the longest x7 75.4 us: contract_rows(): lax.dot_general(left_op, right_op, (((0,), (0,)), ((), ())), preferred_el...]
    ppermute x0 -> x23, waiting for transfers between devices: none -> 45.8 us  [the longest x7 28.8 us: x_go(): lax.ppermute(a, 'dp', [(i, i ^ 1) for i in range(lax.axis_size('dp'))])]
    convert_element_type x9 -> x3, other arithmetic: 44.9 us -> 3.43 us  [the longest x1 2.63 us: shards(): dm_own = (cotangent.astype(F32) * live).astype(BF)]
    reduce_sum x5 -> x0, other arithmetic: 40.1 us -> none  [the longest x2 16.5 us: norm_back(): gain_grad = jnp.sum(upstream * values * inv_rms, axis=0)]
    unnamed x1 -> x0, blocking collectives: 38.8 us -> none
  transfers between devices with their start and end apart: 13 -> 27, of which waited for: 11 -> 6; matrix products, arithmetic and copies ran while one was open for 14% -> 2% of each run, Pallas kernels for 0% -> 59%
where the time goes in v1:
time: 509 us; the launch traced here: 503 us
  Pallas kernels  387 us (76%)
  waiting for transfers between devices  45.9 us (9%)
  local copies, waits for them, and re-layouts  33.3 us (7%)
  starting transfers between devices  15.5 us (3%)
  between operations  14.8 us (3%)
  other arithmetic  6.48 us (1%)
    pallas_call x27, Pallas kernels, call(): pl.pallas_call(wrapped, grid_spec=pltpu.PrefetchScalarGridSpec(num_scalar...  174 us
    pallas_call x1, Pallas kernels, dn2_sum(): pl.pallas_call(body, in_specs=[any_spec] * 8 + [vmem] * 2 + [any_spec] *...  98.5 us
    pallas_call x1, Pallas kernels, front(): pl.pallas_call(front_body, in_specs=[any_spec] * 3 + [vmem] * 2 + [any_sp...  90.6 us
    unnamed x114, local copies, waits for them, and re-layouts  30.6 us
    ppermute x7, waiting for transfers between devices, x_go(): lax.ppermute(a, 'dp', [(i, i ^ 1) for i in range(lax.axis_size('dp'))])  28.8 us
    pallas_call x1, Pallas kernels, gains_sum(): pl.pallas_call(body, in_specs=[vmem] * 2 + [pl.BlockSpec(memory_space=pl....  24 us
    ppermute x6, waiting for transfers between devices, y_go(): return lax.ppermute(a, 'tensor', Y_PERM)  16.2 us
  transfers between devices with their start and end apart: 27, of which 6 were waited for; matrix products, arithmetic and copies ran while one was open for 2% of the time, Pallas kernels for 59%

profile of v1, /device:TPU:0, one launch (start us, length us, event | category | flops | bytes accessed | tf_op | source)
XLA Modules:
  0.0 503.4 jit_solution(2079169080670711113)
XLA Ops:
  7.3 3.0 collective-permute-start.1
  11.0 2.6 multiply_convert_fusion.dm0
  13.6 1.5 collective-permute-start.5
  18.4 16.2 %collective-permute-done.1.refs_2_ = bf16[1024,512]{1,0:T(8,128)(2,1)} collective-permute-done((bf16[1024,512]{1,0:T(8,128)(2,1)}, bf16[1024,512]{1,0:T(8,128)(2,1)}, u32[]{:S(2)}, u32[]{:S(2)}) %collective-permute-start.1) | collective-permute-done | bytes 1048608 | tf_op jit(solution)/shard_map/ppermute | solution.py:39
  34.7 1.9 fusion
  38.6 11.6 %qkv.1 = (bf16[1024,2048]{1,0:T(8,128)(2,1)}, bf16[1024,2048]{1,0:T(8,128)(2,1)}, bf16[1024,1536]{1,0:T(8,128)(2,1)S(1)}) custom-call(s32[5]{0:T(128)S(1)} %stack.23.s, bf16[1024,512]{1,0:T(8,128)(2,1)} %refs_0_.1, bf16[1024,512]{1,0:T(8,128)(2,1)} %collective-permute-done.refs_1_, bf16[1024,512]{1,0:T(8,128)(2,1)} %collective-permute-done.1.refs_2_, ...), custom_call_target="tpu_custom_call" | custom-call | flops 15399999488 | bytes 50400000 | tf_op jit(solution)/shard_map/qkv/pallas_call | solution.py:66
  50.3 15.9 %attention.1 = (bf16[1024,512]{1,0:T(8,128)(2,1)S(1)}, f32[1024,512]{1,0:T(8,128)S(1)}) custom-call(s32[5]{0:T(128)S(1)} %stack.23.s, bf16[1024,1536]{1,0:T(8,128)(2,1)S(1)} %get-tuple-element.51.refs_0_.refs_1_.refs_2_, bf16[1024,1536]{1,0:T(8,128)(2,1)S(1)} %get-tuple-element.51.refs_0_.refs_1_.refs_2_, ...), custom_call_target="tpu_custom_call" | custom-call | flops 18699999232 | bytes 61200000 | tf_op jit(solution)/shard_map/attention/pallas_call | solution.py:66
  67.1 1.3 copy-done.47
  68.5 90.6 %front.1 = (bf16[2048,2048]{1,0:T(8,128)(2,1)}, bf16[2048,1024]{1,0:T(8,128)(2,1)}, bf16[2048,1024]{1,0:T(8,128)(2,1)}, bf16[2048,1024]{1,0:T(8,128)(2,1)}, bf16...) custom-call(bf16[1024,512]{1,0:T(8,128)(2,1)} %copy-done.41, ...), custom_call_target="tpu_custom_call" | custom-call | flops 88000004096 | bytes 288000000 | tf_op jit(solution)/shard_map/front/pallas_call | solution.py:685
  159.1 15.1 %grad.2.refs_2_ = bf16[4,512,2048]{2,1,0:T(8,128)(2,1)} custom-call(s32[5]{0:T(128)} %copy-done.8, bf16[2048,2048]{1,0:T(8,128)(2,1)} %get-tuple-element.59.refs_0_, bf16[2048,1024]{1,0:T(8,128)(2,1)} %get-tuple-element.54.refs_1_), custom_call_target="tpu_custom_call" | custom-call | flops 15399999488 | bytes 50400000 | tf_op jit(solution)/shard_map/grad/pallas_call | solution.py:66
  174.2 14.9 %grad.3.refs_10_ = bf16[4,512,2048]{2,1,0:T(8,128)(2,1)} custom-call(s32[5]{0:T(128)} %copy-done.8, bf16[2048,2048]{1,0:T(8,128)(2,1)} %get-tuple-element.59.refs_0_, bf16[2048,1024]{1,0:T(8,128)(2,1)} %get-tuple-element.55.refs_1_, bf16[4,512,2048]{2,1,0:T(8,128)(2,1)} %grad.2.refs_2_), custom_call_target="tpu_custom_call", output_to_operand_aliasing={{}: (3, {})} | custom-call | flops 15399999488 | bytes 50400000 | tf_op jit(solution)/shard_map/grad/pallas_call | solution.py:66
  189.2 98.5 %dn2_sum.1 = (bf16[1024,2048]{1,0:T(8,128)(2,1)}, f32[256,2048]{1,0:T(8,128)}, f32[1,2048]{1,0:T(1,128)}, f32[256,2048]{1,0:T(8,128)}, bf16[256,2048]{1,0:T(8,128)(2,1)}, /*index=5*/bf16[256,2048]{1,0:T(8,128)(2,1)}) custom-call(bf16[4,2,256,1024]{3,2,1,0:T(8,128)(2,1)} %bitcast.41, bf16[4,2,256,1024]{3,2,1,0:T(8,128)(2,1)} %bitcast.42, ...), custom_call_target="tpu_custom_call" | custom-call | flops 104500002816 | bytes 342000000 | tf_op jit(solution)/shard_map/dn2_sum/pallas_call | solution.py:914
  287.7 1.6 copy-done.14
  289.3 2.2 copy-done.38
  291.5 3.1 dob.1.refs_2_.refs_4_
  295.6 5.5 %pair_grad_send.3.refs_10_ = bf16[4,256,512]{2,1,0:T(8,128)(2,1)} custom-call(s32[5]{0:T(128)} %copy-done.8, bf16[1024,2048]{1,0:T(8,128)(2,1)} %get-tuple-element.63.refs_0_, bf16[1024,512]{1,0:T(8,128)(2,1)} %copy-done.41, bf16[1024,512]{1,0:T(8,128)(2,1)} %copy-done.42), custom_call_target="tpu_custom_call" | custom-call | flops 5500000256 | bytes 18000000 | tf_op jit(solution)/shard_map/pair_grad_send/pallas_call | solution.py:66
  301.5 13.8 %attention_back.2 = (bf16[1024,256]{1,0:T(8,128)(2,1)}, bf16[1024,256]{1,0:T(8,128)(2,1)}, bf16[1024,256]{1,0:T(8,128)(2,1)}) custom-call(s32[5]{0:T(128)} %copy-done.8, bf16[1024,1536]{1,0:T(8,128)(2,1)} %copy-done.43, bf16[1024,1536]{1,0:T(8,128)(2,1)} %copy-done.43, bf16[1024,1536]{1,0:T(8,128)(2,1)} %copy-done.43, bf16[1024,512]{1,0:T(8,128)(2,1)} %copy-done.41, ...), custom_call_target="tpu_custom_call" | custom-call | flops 14300000256 | bytes 46800000 | tf_op jit(solution)/shard_map/attention_back/pallas_call | solution.py:66
  315.4 6.5 %pair_grad_send.4.refs_1_ = bf16[4,256,768]{2,1,0:T(8,128)(2,1)} custom-call(s32[5]{0:T(128)} %copy-done.8, bf16[1024,2048]{1,0:T(8,128)(2,1)} %get-tuple-element.62.refs_0_, bf16[1024,256]{1,0:T(8,128)(2,1)} %get-tuple-element.65.refs_1_.refs_0_, bf16[1024,256]{1,0:T(8,128)(2,1)} %get-tuple-element.66.refs_2_.refs_1_, ...), custom_call_target="tpu_custom_call" | custom-call | flops 5500000256 | bytes 18000000 | tf_op jit(solution)/shard_map/pair_grad_send/pallas_call | solution.py:66
  321.8 1.6 collective-permute-start.9
  323.4 1.4 copy-done.20
  326.4 14.2 %attention_back.3 = (bf16[1024,256]{1,0:T(8,128)(2,1)}, bf16[1024,256]{1,0:T(8,128)(2,1)}, bf16[1024,256]{1,0:T(8,128)(2,1)}) custom-call(s32[5]{0:T(128)} %copy-done.8, bf16[1024,1536]{1,0:T(8,128)(2,1)} %copy-done.43, bf16[1024,1536]{1,0:T(8,128)(2,1)} %copy-done.43, bf16[1024,1536]{1,0:T(8,128)(2,1)} %copy-done.43, bf16[1024,512]{1,0:T(8,128)(2,1)} %copy-done.41, ...), custom_call_target="tpu_custom_call" | custom-call | flops 14300000256 | bytes 46800000 | tf_op jit(solution)/shard_map/attention_back/pallas_call | solution.py:66
  341.9 6.1 %pair_grad_send.5.refs_3_ = bf16[4,256,768]{2,1,0:T(8,128)(2,1)} custom-call(s32[5]{0:T(128)} %copy-done.8, bf16[1024,2048]{1,0:T(8,128)(2,1)} %get-tuple-element.62.refs_0_, bf16[1024,256]{1,0:T(8,128)(2,1)} %get-tuple-element.69.refs_1_.refs_3_, bf16[1024,256]{1,0:T(8,128)(2,1)} %get-tuple-element.70.refs_2_.refs_4_, ...), custom_call_target="tpu_custom_call" | custom-call | flops 5500000256 | bytes 18000000 | tf_op jit(solution)/shard_map/pair_grad_send/pallas_call | solution.py:66
  349.0 5.7 %pair_grad_keep.3.refs_5_.refs_6_ = bf16[4,256,512]{2,1,0:T(8,128)(2,1)} custom-call(s32[5]{0:T(128)} %copy-done.8, bf16[1024,2048]{1,0:T(8,128)(2,1)} %get-tuple-element.63.refs_0_, bf16[1024,512]{1,0:T(8,128)(2,1)} %copy-done.41, bf16[4,256,512]{2,1,0:T(8,128)(2,1)} %copy-done.54, bf16[4,256,768]{2,1,0:T(8,128)(2,1)} %pair_grad_send.5.refs_3_), custom_call_target="tpu_custom_call" | custom-call | flops 5500000256 | bytes 18000000 | tf_op jit(solution)/shard_map/pair_grad_keep/pallas_call | solution.py:66
  354.7 6.3 %collective-permute-done.9.refs_4_ = bf16[4,256,768]{2,1,0:T(8,128)(2,1)S(1)} collective-permute-done((bf16[4,256,768]{2,1,0:T(8,128)(2,1)}, bf16[4,256,768]{2,1,0:T(8,128)(2,1)S(1)}, u32[]{:S(2)}, u32[]{:S(2)}) %collective-permute-start.9) | collective-permute-done | bytes 1572896 | tf_op jit(solution)/shard_map/ppermute | solution.py:47
  362.2 7.0 %pair_grad_keep.4.refs_5_ = bf16[4,256,1280]{2,1,0:T(8,128)(2,1)} custom-call(s32[5]{0:T(128)} %copy-done.8, bf16[1024,2048]{1,0:T(8,128)(2,1)} %get-tuple-element.62.refs_0_, bf16[1024,256]{1,0:T(8,128)(2,1)} %get-tuple-element.65.refs_1_.refs_0_, bf16[1024,256]{1,0:T(8,128)(2,1)} %get-tuple-element.66.refs_2_.refs_1_, ...), custom_call_target="tpu_custom_call" | custom-call | flops 6600000000 | bytes 21600000 | tf_op jit(solution)/shard_map/pair_grad_keep/pallas_call | solution.py:66
  369.3 13.5 %collective-permute-done.7.refs_1_ = bf16[256,2048]{1,0:T(8,128)(2,1)} collective-permute-done((bf16[256,2048]{1,0:T(8,128)(2,1)}, bf16[256,2048]{1,0:T(8,128)(2,1)}, u32[]{:S(2)}, u32[]{:S(2)}) %collective-permute-start.7) | collective-permute-done | bytes 1048608 | tf_op jit(solution)/shard_map/ppermute | solution.py:47
  382.8 1.6 copy-done.39
  384.4 1.6 copy-done.40
  386.0 3.1 layer_rows.1
  391.2 9.1 %tensor_send.1 = (bf16[256,2048]{1,0:T(8,128)(2,1)}, bf16[256,2048]{1,0:T(8,128)(2,1)}) custom-call(s32[5]{0:T(128)} %copy-done.8, bf16[1024,256]{1,0:T(8,128)(2,1)} %get-tuple-element.65.refs_1_.refs_0_, bf16[1024,256]{1,0:T(8,128)(2,1)} %get-tuple-element.66.refs_2_.refs_1_, bf16[1024,256]{1,0:T(8,128)(2,1)} %get-tuple-element.67.refs_3_.refs_2_, ...), custom_call_target="tpu_custom_call" | custom-call | flops 7699999744 | bytes 25200000 | tf_op jit(solution)/shard_map/tensor_send/pallas_call | solution.py:66
  404.2 6.9 %tensor_far.1.refs_1_ = bf16[256,2048]{1,0:T(8,128)(2,1)} custom-call(s32[5]{0:T(128)} %copy-done.8, bf16[1024,256]{1,0:T(8,128)(2,1)} %get-tuple-element.65.refs_1_.refs_0_, bf16[1024,256]{1,0:T(8,128)(2,1)} %get-tuple-element.66.refs_2_.refs_1_, bf16[1024,256]{1,0:T(8,128)(2,1)} %get-tuple-element.67.refs_3_.refs_2_, ...), custom_call_target="tpu_custom_call" | custom-call | flops 7699999744 | bytes 25200000 | tf_op jit(solution)/shard_map/tensor_far/pallas_call | solution.py:66
  411.1 1.2 copy-done.21
  413.6 1.4 pair_send.2.refs_1_
  415.0 1.6 copy-done.18
  420.2 2.7 place.2.refs_13_
  422.9 7.1 %tensor_near.1.refs_5_.refs_0_ = f32[256,2048]{1,0:T(8,128)} custom-call(s32[5]{0:T(128)} %copy-done.8, bf16[1024,256]{1,0:T(8,128)(2,1)} %get-tuple-element.65.refs_1_.refs_0_, bf16[1024,256]{1,0:T(8,128)(2,1)} %get-tuple-element.66.refs_2_.refs_1_, bf16[1024,256]{1,0:T(8,128)(2,1)} %get-tuple-element.67.refs_3_.refs_2_, ...), custom_call_target="tpu_custom_call" | custom-call | flops 7699999744 | bytes 25200000 | tf_op jit(solution)/shard_map/tensor_near/pallas_call | solution.py:66
  430.0 8.0 %collective-permute-done.17.refs_4_ = bf16[4,256,768]{2,1,0:T(8,128)(2,1)} collective-permute-done((bf16[4,256,768]{2,1,0:T(8,128)(2,1)}, bf16[4,256,768]{2,1,0:T(8,128)(2,1)}, u32[]{:S(2)}, u32[]{:S(2)}) %collective-permute-start.17) | collective-permute-done | bytes 1572896 | tf_op jit(solution)/shard_map/ppermute | solution.py:47
  438.0 6.4 %pair_grad_keep.5.refs_5_ = bf16[4,256,768]{2,1,0:T(8,128)(2,1)} custom-call(s32[5]{0:T(128)} %copy-done.8, bf16[1024,2048]{1,0:T(8,128)(2,1)} %get-tuple-element.62.refs_0_, bf16[1024,256]{1,0:T(8,128)(2,1)} %get-tuple-element.69.refs_1_.refs_3_, bf16[1024,256]{1,0:T(8,128)(2,1)} %get-tuple-element.70.refs_2_.refs_4_, ...), custom_call_target="tpu_custom_call" | custom-call | flops 5500000256 | bytes 18000000 | tf_op jit(solution)/shard_map/pair_grad_keep/pallas_call | solution.py:66
  444.4 6.3 %norm1_back.1 = (bf16[256,512]{1,0:T(8,128)(2,1)}, bf16[256,512]{1,0:T(8,128)(2,1)}, bf16[256,512]{1,0:T(8,128)(2,1)}, bf16[256,512]{1,0:T(8,128)(2,1)}, f32[1,2048]{1,0:T(1,128)}) custom-call(s32[5]{0:T(128)} %copy-done.8, f32[256,2048]{1,0:T(8,128)} %tensor_near.1.refs_5_.refs_0_, bf16[256,2048]{1,0:T(8,128)(2,1)} %collective-permute-done.16.refs_1_, ...), custom_call_target="tpu_custom_call" | custom-call | flops 6600000000 | bytes 21600000 | tf_op jit(solution)/shard_map/norm1_back/pallas_call | solution.py:66
  451.0 1.6 collective-permute-start.20
  453.3 24.0 %gains.1.refs_2_ = f32[2,2048]{1,0:T(2,128)S(1)} custom-call(f32[1,2048]{1,0:T(1,128)S(1)} %copy-done.48, f32[1,2048]{1,0:T(1,128)S(1)} %copy-done.49), custom_call_target="tpu_custom_call" | custom-call | flops 13200000000 | bytes 43200000 | tf_op jit(solution)/shard_map/gains/pallas_call | solution.py:1117
  478.0 2.7 pair_join.2
  480.7 1.6 copy-done.33
  482.3 3.0 pair_join.3.refs_1_
  486.4 1.6 copy-done.34
  488.0 1.5 flip.1.refs_5_
  490.6 1.8 place.3.refs_2_
  494.6 1.7 head_halves.1
  (171 shorter events, 30.5 us)
Async XLA Ops:
  7.2 9.0 %copy-start.56 = (s32[8]{0:T(128)S(1)}, s32[8]{0:T(128)}, u32[]{:S(2)}) copy-start(s32[8]{0:T(128)} %param.24) | copy-start | bytes 100
  7.2 9.2 %copy-start.50 = (bf16[2048]{0:T(1024)(128)(2,1)S(1)}, bf16[2048]{0:T(1024)(128)(2,1)}, u32[]{:S(2)}) copy-start(bf16[2048]{0:T(1024)(128)(2,1)} %param.14) | copy-start | bytes 12292
  7.2 9.2 %copy-start.51 = (bf16[2048]{0:T(1024)(128)(2,1)S(1)}, bf16[2048]{0:T(1024)(128)(2,1)}, u32[]{:S(2)}) copy-start(bf16[2048]{0:T(1024)(128)(2,1)} %param.19) | copy-start | bytes 12292
  7.2 403.9 %reduce-scatter.7.cloned.1.call-start = ((), (), s32[]{:S(2)}) async-start(), calls=%async_computation.5 | async-start | bytes 5242880 | tf_op jit(solution)/shard_map/reduce_scatter | solution.py:968
  7.3 27.3 %collective-permute-start.1 = (bf16[1024,512]{1,0:T(8,128)(2,1)}, bf16[1024,512]{1,0:T(8,128)(2,1)}, u32[]{:S(2)}, u32[]{:S(2)}) collective-permute-start(bf16[1024,512]{1,0:T(8,128)(2,1)} %refs_0_.1), channel_id=1, source_target_pairs={{0,2},{2,0},{1,3},{3,1},{4,6},{6,4},{5,7},{7,5},{8,10},{10,8},{9,1... | collective-permute-start | bytes 3145736 | tf_op jit(solution)/shard_map/ppermute | solution.py:39
  11.0 27.6 %copy-start.17 = (bf16[2048,512]{1,0:T(8,128)(2,1)S(1)}, bf16[2048,512]{1,0:T(8,128)(2,1)}, u32[]{:S(2)}) copy-start(bf16[2048,512]{1,0:T(8,128)(2,1)} %refs_11_.5) | copy-start | bytes 6291460
  13.6 24.9 %collective-permute-start.5 = (bf16[1024,512]{1,0:T(8,128)(2,1)}, bf16[1024,512]{1,0:T(8,128)(2,1)}, u32[]{:S(2)}, u32[]{:S(2)}) collective-permute-start(bf16[1024,512]{1,0:T(8,128)(2,1)} %multiply_convert_fusion.dm0), channel_id=1, source_target_pairs={{0,4},{4,0},{8,12},{12,8},{16,20},{20,16},{24,28},{28,24},{1,5},{5... | collective-permute-start | bytes 3145736 | tf_op jit(solution)/shard_map/ppermute | solution.py:47
  15.1 53.3 %collective-permute-start.4 = (bf16[1024,512]{1,0:T(8,128)(2,1)}, bf16[1024,512]{1,0:T(8,128)(2,1)}, u32[]{:S(2)}, u32[]{:S(2)}) collective-permute-start(bf16[1024,512]{1,0:T(8,128)(2,1)} %multiply_convert_fusion.dm0), channel_id=1, source_target_pairs={{0,2},{2,0},{1,3},{3,1},{4,6},{6,4},{5,7},{7,5},{8,10},{10,8},{9,1... | collective-permute-start | bytes 3145736 | tf_op jit(solution)/shard_map/ppermute | solution.py:39
  15.6 52.8 %collective-permute-start.3 = (bf16[1024,512]{1,0:T(8,128)(2,1)}, bf16[1024,512]{1,0:T(8,128)(2,1)}, u32[]{:S(2)}, u32[]{:S(2)}) collective-permute-start(bf16[1024,512]{1,0:T(8,128)(2,1)} %multiply_convert_fusion.dm0), channel_id=1, source_target_pairs={{0,1},{1,0},{2,3},{3,2},{4,5},{5,4},{6,7},{7,6},{8,9},{9,8},{10,11... | collective-permute-start | bytes 3145736 | tf_op jit(solution)/shard_map/ppermute | solution.py:35
  15.6 22.9 %collective-permute-start = (bf16[1024,512]{1,0:T(8,128)(2,1)}, bf16[1024,512]{1,0:T(8,128)(2,1)}, u32[]{:S(2)}, u32[]{:S(2)}) collective-permute-start(bf16[1024,512]{1,0:T(8,128)(2,1)} %refs_0_.1), channel_id=1, source_target_pairs={{0,1},{1,0},{2,3},{3,2},{4,5},{5,4},{6,7},{7,6},{8,9},{9,8},{10,11... | collective-permute-start | bytes 3145736 | tf_op jit(solution)/shard_map/ppermute | solution.py:35
  16.4 22.2 %copy-start.6 = (bf16[1,2048]{1,0:T(2,128)(2,1)}, bf16[1,2048]{1,0:T(2,128)(2,1)S(1)}, u32[]{:S(2)}) copy-start(bf16[1,2048]{1,0:T(2,128)(2,1)S(1)} %broadcast_in_dim.9.refs_4_.refs_3_) | copy-start | bytes 12292
  18.3 31.9 %copy-start.5 = (s32[1024,1]{1,0:T(8,128)}, s32[1024,1]{1,0:T(8,128)S(1)}, u32[]{:S(2)}) copy-start(s32[1024,1]{1,0:T(8,128)S(1)} %copy.32.refs_3_.refs_6_) | copy-start | bytes 12292
  18.4 31.8 %copy-start.8 = (s32[5]{0:T(128)}, s32[5]{0:T(128)S(1)}, u32[]{:S(2)}) copy-start(s32[5]{0:T(128)S(1)} %stack.23.s) | copy-start | bytes 64
  34.6 4.0 collective-permute-start.2
  37.5 12.7 %copy-start.2 = (f32[1024,128]{1,0:T(8,128)}, f32[1024,128]{1,0:T(8,128)S(1)}, u32[]{:S(2)}) copy-start(f32[1024,128]{1,0:T(8,128)S(1)} %get-tuple-element.98.refs_8_) | copy-start | bytes 1572868
  37.5 12.7 %copy-start.3 = (f32[1024,128]{1,0:T(8,128)}, f32[1024,128]{1,0:T(8,128)S(1)}, u32[]{:S(2)}) copy-start(f32[1024,128]{1,0:T(8,128)S(1)} %get-tuple-element.99.refs_9_) | copy-start | bytes 1572868
  37.6 12.7 %copy-start.7 = (s32[8,128]{1,0:T(8,128)}, s32[8,128]{1,0:T(8,128)S(1)}, u32[]{:S(2)}) copy-start(s32[8,128]{1,0:T(8,128)S(1)} %fusion.2) | copy-start | bytes 12292
  38.6 29.9 %collective-permute-start.6 = (bf16[1024,512]{1,0:T(8,128)(2,1)}, bf16[1024,512]{1,0:T(8,128)(2,1)}, u32[]{:S(2)}, u32[]{:S(2)}) collective-permute-start(bf16[1024,512]{1,0:T(8,128)(2,1)} %collective-permute-done.5.dmx), channel_id=1, source_target_pairs={{0,1},{1,0},{2,3},{3,2},{4,5},{5,4},{6,7},{7,6},{8,9},{9,8},{10,11... | collective-permute-start | bytes 3145736 | tf_op jit(solution)/shard_map/ppermute | solution.py:35
  50.2 15.9 %copy-start.43 = (bf16[1024,1536]{1,0:T(8,128)(2,1)}, bf16[1024,1536]{1,0:T(8,128)(2,1)S(1)}, u32[]{:S(2)}) copy-start(bf16[1024,1536]{1,0:T(8,128)(2,1)S(1)} %get-tuple-element.51.refs_0_.refs_1_.refs_2_) | copy-start | bytes 9437188
  159.0 255.9 %reduce-scatter.5.cloned.1.call-start = ((), (), s32[]{:S(2)}) async-start(), calls=%async_computation.4 | async-start | bytes 10485760 | tf_op jit(solution)/shard_map/reduce_scatter | solution.py:968
  189.1 296.2 %reduce-scatter.9.cloned.1.call-start = ((), (), s32[]{:S(2)}) async-start(), calls=%async_computation.6 | async-start | bytes 3276800 | tf_op jit(solution)/shard_map/reduce_scatter | solution.py:968
  189.2 98.6 %copy-start.9 = (s32[5]{0:T(128)S(1)}, s32[5]{0:T(128)}, u32[]{:S(2)}) copy-start(s32[5]{0:T(128)} %copy-done.8) | copy-start | bytes 64
  301.1 46.9 %collective-permute-start.10 = (bf16[4,256,512]{2,1,0:T(8,128)(2,1)}, bf16[4,256,512]{2,1,0:T(8,128)(2,1)S(1)}, u32[]{:S(2)}, u32[]{:S(2)}) collective-permute-start(bf16[4,256,512]{2,1,0:T(8,128)(2,1)} %pair_grad_send.3.refs_10_), channel_id=1, source_target_pairs={{0,4},{4,0},{8,12},{12,8},{16,20},{20,16},{24,28},{28,24},{1,5},{5... | collective-permute-start | bytes 3145736 | tf_op jit(solution)/shard_map/ppermute | solution.py:47
  315.3 8.1 %copy-start.10 = (s32[5]{0:T(128)S(1)}, s32[5]{0:T(128)}, u32[]{:S(2)}) copy-start(s32[5]{0:T(128)} %copy-done.8) | copy-start | bytes 64
  321.8 39.2 %collective-permute-start.9 = (bf16[4,256,768]{2,1,0:T(8,128)(2,1)}, bf16[4,256,768]{2,1,0:T(8,128)(2,1)S(1)}, u32[]{:S(2)}, u32[]{:S(2)}) collective-permute-start(bf16[4,256,768]{2,1,0:T(8,128)(2,1)} %pair_grad_send.4.refs_1_), channel_id=1, source_target_pairs={{0,4},{4,0},{8,12},{12,8},{16,20},{20,16},{24,28},{28,24},{1,5},{5... | collective-permute-start | bytes 4718600 | tf_op jit(solution)/shard_map/ppermute | solution.py:47
  340.6 42.2 %collective-permute-start.7 = (bf16[256,2048]{1,0:T(8,128)(2,1)}, bf16[256,2048]{1,0:T(8,128)(2,1)}, u32[]{:S(2)}, u32[]{:S(2)}) collective-permute-start(bf16[256,2048]{1,0:T(8,128)(2,1)} %copy-done.25), channel_id=1, source_target_pairs={{0,4},{4,0},{8,12},{12,8},{16,20},{20,16},{24,28},{28,24},{1,5},{5... | collective-permute-start | bytes 3145736 | tf_op jit(solution)/shard_map/ppermute | solution.py:47
  341.1 28.2 %collective-permute-start.8 = (bf16[256,2048]{1,0:T(8,128)(2,1)}, bf16[256,2048]{1,0:T(8,128)(2,1)}, u32[]{:S(2)}, u32[]{:S(2)}) collective-permute-start(bf16[256,2048]{1,0:T(8,128)(2,1)} %get-tuple-element.68), channel_id=1, source_target_pairs={{0,2},{2,0},{1,3},{3,1},{4,6},{6,4},{5,7},{7,5},{8,10},{10,8},{9,1... | collective-permute-start | bytes 3145736 | tf_op jit(solution)/shard_map/ppermute | solution.py:39
  362.2 20.6 %copy-start.4 = (f32[1024,1]{1,0:T(8,128)S(1)}, f32[1024,1]{1,0:T(8,128)}, u32[]{:S(2)}) copy-start(f32[1024,1]{1,0:T(8,128)} %copy.33.live.refs_8_.refs_4_) | copy-start | bytes 12292
  369.2 13.6 %copy-start = (bf16[4,256,1280]{2,1,0:T(8,128)(2,1)S(1)}, bf16[4,256,1280]{2,1,0:T(8,128)(2,1)}, u32[]{:S(2)}) copy-start(bf16[4,256,1280]{2,1,0:T(8,128)(2,1)} %pair_grad_keep.4.refs_5_) | copy-start | bytes 7864324
  369.2 13.6 %copy-start.11 = (s32[5]{0:T(128)S(1)}, s32[5]{0:T(128)}, u32[]{:S(2)}) copy-start(s32[5]{0:T(128)} %copy-done.8) | copy-start | bytes 64
  369.2 123.2 %reduce-scatter.11.cloned.1.call-start = ((), (), s32[]{:S(2)}) async-start(), calls=%async_computation.7 | async-start | bytes 1966080 | tf_op jit(solution)/shard_map/reduce_scatter | solution.py:968
  391.2 9.3 %copy-start.32 = (bf16[256,512]{1,0:T(8,128)(2,1)S(1)}, bf16[256,512]{1,0:T(8,128)(2,1)}, u32[]{:S(2)}) copy-start(bf16[256,512]{1,0:T(8,128)(2,1)} %copy-done.31) | copy-start | bytes 786436
  391.2 9.7 %copy-start.30 = (bf16[256,512]{1,0:T(8,128)(2,1)S(1)}, bf16[256,512]{1,0:T(8,128)(2,1)}, u32[]{:S(2)}) copy-start(bf16[256,512]{1,0:T(8,128)(2,1)} %copy-done.29) | copy-start | bytes 786436
  400.3 2.9 collective-permute-start.14
  400.4 37.6 %collective-permute-start.17 = (bf16[4,256,768]{2,1,0:T(8,128)(2,1)}, bf16[4,256,768]{2,1,0:T(8,128)(2,1)}, u32[]{:S(2)}, u32[]{:S(2)}) collective-permute-start(bf16[4,256,768]{2,1,0:T(8,128)(2,1)} %pair_grad_send.5.refs_3_), channel_id=1, source_target_pairs={{0,4},{4,0},{8,12},{12,8},{16,20},{20,16},{24,28},{28,24},{1,5},{5... | collective-permute-start | bytes 4718600 | tf_op jit(solution)/shard_map/ppermute | solution.py:47
  400.5 16.8 %collective-permute-start.11 = (bf16[256,512]{1,0:T(8,128)(2,1)S(1)}, bf16[256,512]{1,0:T(8,128)(2,1)}, u32[]{:S(2)}, u32[]{:S(2)}) collective-permute-start(bf16[256,512]{1,0:T(8,128)(2,1)S(1)} %copy-done.32), channel_id=1, source_target_pairs={{0,1},{1,0},{2,3},{3,2},{4,5},{5,4},{6,7},{7,6},{8,9},{9,8},{10,11... | collective-permute-start | bytes 786440 | tf_op jit(solution)/shard_map/ppermute | solution.py:35
  400.9 17.3 %collective-permute-start.12 = (bf16[256,512]{1,0:T(8,128)(2,1)S(1)}, bf16[256,512]{1,0:T(8,128)(2,1)}, u32[]{:S(2)}, u32[]{:S(2)}) collective-permute-start(bf16[256,512]{1,0:T(8,128)(2,1)S(1)} %copy-done.30), channel_id=1, source_target_pairs={{0,2},{2,0},{1,3},{3,1},{4,6},{6,4},{5,7},{7,5},{8,10},{10,8},{9,1... | collective-permute-start | bytes 786440 | tf_op jit(solution)/shard_map/ppermute | solution.py:39
  401.5 17.9 %collective-permute-start.13 = (bf16[256,512]{1,0:T(8,128)(2,1)S(1)}, bf16[256,512]{1,0:T(8,128)(2,1)}, u32[]{:S(2)}, u32[]{:S(2)}) collective-permute-start(bf16[256,512]{1,0:T(8,128)(2,1)S(1)} %get-tuple-element.75), channel_id=1, source_target_pairs={{0,3},{3,0},{1,2},{2,1},{4,7},{7,4},{5,6},{6,5},{8,11},{11,8},{9,1... | collective-permute-start | bytes 786440 | tf_op jit(solution)/shard_map/ppermute | solution.py:43
  403.3 19.7 %collective-permute-start.15 = (bf16[256,2048]{1,0:T(8,128)(2,1)}, bf16[256,2048]{1,0:T(8,128)(2,1)}, u32[]{:S(2)}, u32[]{:S(2)}) collective-permute-start(bf16[256,2048]{1,0:T(8,128)(2,1)} %get-tuple-element.78), channel_id=1, source_target_pairs={{0,1},{1,0},{2,3},{3,2},{4,5},{5,4},{6,7},{7,6},{8,9},{9,8},{10,11... | collective-permute-start | bytes 3145736 | tf_op jit(solution)/shard_map/ppermute | solution.py:35
  417.8 26.6 %collective-permute-start.16 = (bf16[256,2048]{1,0:T(8,128)(2,1)S(1)}, bf16[256,2048]{1,0:T(8,128)(2,1)}, u32[]{:S(2)}, u32[]{:S(2)}) collective-permute-start(bf16[256,2048]{1,0:T(8,128)(2,1)S(1)} %copy-done.24), channel_id=1, source_target_pairs={{0,2},{2,0},{1,3},{3,1},{4,6},{6,4},{5,7},{7,5},{8,10},{10,8},{9,1... | collective-permute-start | bytes 3145736 | tf_op jit(solution)/shard_map/ppermute | solution.py:39
  418.2 62.5 %collective-permute-start.21 = (bf16[1024,256]{1,0:T(8,128)(2,1)}, bf16[1024,256]{1,0:T(8,128)(2,1)}, u32[]{:S(2)}, u32[]{:S(2)}) collective-permute-start(bf16[1024,256]{1,0:T(8,128)(2,1)} %pair_send.2.refs_1_), channel_id=1, source_target_pairs={{0,4},{4,0},{8,12},{12,8},{16,20},{20,16},{24,28},{28,24},{1,5},{5... | collective-permute-start | bytes 1572872 | tf_op jit(solution)/shard_map/ppermute | solution.py:47
  419.4 58.6 %collective-permute-start.22 = (bf16[256,2048]{1,0:T(8,128)(2,1)S(1)}, bf16[256,2048]{1,0:T(8,128)(2,1)S(1)}, u32[]{:S(2)}, u32[]{:S(2)}) collective-permute-start(bf16[256,2048]{1,0:T(8,128)(2,1)S(1)} %pair_send.3.refs_4_), channel_id=1, source_target_pairs={{0,4},{4,0},{8,12},{12,8},{16,20},{20,16},{24,28},{28,24},{1,5},{5... | collective-permute-start | bytes 3145736 | tf_op jit(solution)/shard_map/ppermute | solution.py:47
  444.4 8.2 %copy-start.49 = (f32[1,2048]{1,0:T(1,128)S(1)}, f32[1,2048]{1,0:T(1,128)}, u32[]{:S(2)}) copy-start(f32[1,2048]{1,0:T(1,128)} %get-tuple-element.85.two) | copy-start | bytes 24580
  450.7 38.8 %collective-permute-start.18 = (bf16[256,512]{1,0:T(8,128)(2,1)}, bf16[256,512]{1,0:T(8,128)(2,1)S(1)}, u32[]{:S(2)}, u32[]{:S(2)}) collective-permute-start(bf16[256,512]{1,0:T(8,128)(2,1)} %get-tuple-element.81), channel_id=1, source_target_pairs={{0,1},{1,0},{2,3},{3,2},{4,5},{5,4},{6,7},{7,6},{8,9},{9,8},{10,11... | collective-permute-start | bytes 786440 | tf_op jit(solution)/shard_map/ppermute | solution.py:35
  450.7 38.8 %collective-permute-start.19 = (bf16[256,512]{1,0:T(8,128)(2,1)}, bf16[256,512]{1,0:T(8,128)(2,1)S(1)}, u32[]{:S(2)}, u32[]{:S(2)}) collective-permute-start(bf16[256,512]{1,0:T(8,128)(2,1)} %get-tuple-element.82), channel_id=1, source_target_pairs={{0,2},{2,0},{1,3},{3,1},{4,6},{6,4},{5,7},{7,5},{8,10},{10,8},{9,1... | collective-permute-start | bytes 786440 | tf_op jit(solution)/shard_map/ppermute | solution.py:39
  451.0 38.5 %collective-permute-start.20 = (bf16[256,512]{1,0:T(8,128)(2,1)}, bf16[256,512]{1,0:T(8,128)(2,1)S(1)}, u32[]{:S(2)}, u32[]{:S(2)}) collective-permute-start(bf16[256,512]{1,0:T(8,128)(2,1)} %get-tuple-element.83), channel_id=1, source_target_pairs={{0,3},{3,0},{1,2},{2,1},{4,7},{7,4},{5,6},{6,5},{8,11},{11,8},{9,1... | collective-permute-start | bytes 786440 | tf_op jit(solution)/shard_map/ppermute | solution.py:43
  453.3 24.7 %copy-start.13 = (s32[5]{0:T(128)S(1)}, s32[5]{0:T(128)}, u32[]{:S(2)}) copy-start(s32[5]{0:T(128)} %copy-done.8) | copy-start | bytes 64
  453.3 24.7 %copy-start.19 = (bf16[1,512,2048]{2,1,0:T(8,128)(2,1)S(1)}, bf16[1,512,2048]{2,1,0:T(8,128)(2,1)}, u32[]{:S(2)}) copy-start(bf16[1,512,2048]{2,1,0:T(8,128)(2,1)} %reduce-scatter.5.cloned.1.call-done) | copy-start | bytes 6291460
  (36 other events, 69.2 us)
Sparse Core Ops, SparseCore 0:
  159.2 77.7 reduce-scatter.6
  239.4 144.9 reduce-scatter.4
  386.8 52.8 reduce-scatter.8
  444.5 35.5 reduce-scatter.10

commit v2 on v1

--- a/solution.py
+++ b/solution.py
@@ -159,12 +159,18 @@
     return jnp.where(lane if h == 0 else jnp.logical_not(lane), v, jnp.zeros_like(v))
 
 
-def attn_body(s, q_ref, k_ref, v_ref, seq_ref, key_ref, o_ref, lse_ref, *, blk):
+def attn_body(s, q_ref, k_ref, v_ref, seq_ref, key_ref, o_ref, lse_ref, mask, *, blk):
     slots = q_ref.shape[0]
+
+    @pl.when(pl.program_id(0) == 0)
+    def _():
+        for first in range(0, slots, blk):
+            mask[first : first + blk, : first + blk] = mask_bias(seq_ref, key_ref, first, blk)
+
     lane = lax.broadcasted_iota(jnp.int32, (blk, 128), 1) < HD
     for i in range(slots // blk):
         first, n = i * blk, (i + 1) * blk
-        bias = mask_bias(seq_ref, key_ref, first, blk)
+        bias = mask[first:n, :n]
         q2 = q_ref[first:n, :] * jnp.asarray(0.125, BF)
         k2 = k_ref[:n, :]
         v2 = v_ref[:n, :]
@@ -195,6 +201,7 @@
         + [(seq_col, (slots, 1), fixed(0, 0)), (key_row, (1, slots), fixed(0, 0))],
         [(sds((slots, width), d), (slots, 128), third(0)) for d in (BF, F32)],
         deps,
+        scratch=[pltpu.VMEM((slots, slots), F32)],
         limit=24,
     )
 
@@ -1243,13 +1250,13 @@
     first_sum, last_sum = line_sum(first_parts), line_sum(last_parts)
     *in_parts, grad_one = norm1_back(scal, near, y_go(far), x_full, gain_one, back_two, (last,))
     in_pieces = to_features(in_parts)
-    all_gains = gains_sum(grad_one, grad_two, lines, ())
+    part = back_a[0].shape[1]
+    out_grad = flip(scal, first_sum, 3 * part, 2 * part, (grad_one,))
+    down_grad = pair_join(scal, down_sum, x_go(down_send), 1, 1, (out_grad,))
+    all_gains = gains_sum(grad_one, grad_two, lines, (down_grad,))
+    gains = lax.dynamic_slice_in_dim(all_gains, d * rows_dp, rows_dp, 1)
     gate_grad, up_grad = pair_join(scal, ups_sum, x_go(ups_send), 0, 2, (all_gains,))
-    down_grad = pair_join(scal, down_sum, x_go(down_send), 1, 1, (gate_grad,))
-    gains = lax.dynamic_slice_in_dim(all_gains, d * rows_dp, rows_dp, 1)
-    part = back_a[0].shape[1]
-    out_grad = flip(scal, first_sum, 3 * part, 2 * part, (down_grad,))
-    input_grad = place_rows(scal, in_pieces, cotangent, (out_grad,))
+    input_grad = place_rows(scal, in_pieces, cotangent, (gate_grad,))
     query_grad, key_grad, value_grad = head_halves(scal, first_sum, last_sum, part, (input_grad,))
     return (
         layer_out,

time: 509 us -> 500 us (0.982)
  Pallas kernels: 387 us -> 378 us
    pallas_call x1, Pallas kernels: 24 us -> 15.7 us  [gains_sum(): pl.pallas_call(body, in_specs=[vmem] * 2 + [pl.BlockSpec(memory_space=pl....]
    unnamed x114 -> x116, local copies, waits for them, and re-layouts: 30.6 us -> 30.7 us
  transfers between devices with their start and end apart: 27 -> 27, of which waited for: 6 -> 6; matrix products, arithmetic and copies ran while one was open for 2% -> 2% of each run, Pallas kernels for 59% -> 58%
where the time goes in v2:
time: 500 us; the launch traced here: 494 us
  Pallas kernels  378 us (76%)
  waiting for transfers between devices  45.9 us (9%)
  local copies, waits for them, and re-layouts  33.3 us (7%)
  starting transfers between devices  15.5 us (3%)
  between operations  14.8 us (3%)
  other arithmetic  6.48 us (1%)
    pallas_call x27, Pallas kernels, call(): pl.pallas_call(wrapped, grid_spec=pltpu.PrefetchScalarGridSpec(num_scalar...  174 us
    pallas_call x1, Pallas kernels, dn2_sum(): pl.pallas_call(body, in_specs=[any_spec] * 8 + [vmem] * 2 + [any_spec] *...  98.5 us
    pallas_call x1, Pallas kernels, front(): pl.pallas_call(front_body, in_specs=[any_spec] * 3 + [vmem] * 2 + [any_sp...  90.5 us
    unnamed x116, local copies, waits for them, and re-layouts  30.7 us
    ppermute x7, waiting for transfers between devices, x_go(): lax.ppermute(a, 'dp', [(i, i ^ 1) for i in range(lax.axis_size('dp'))])  28.8 us
    ppermute x6, waiting for transfers between devices, y_go(): return lax.ppermute(a, 'tensor', Y_PERM)  16.2 us
    pallas_call x1, Pallas kernels, gains_sum(): pl.pallas_call(body, in_specs=[vmem] * 2 + [pl.BlockSpec(memory_space=pl....  15.7 us
  transfers between devices with their start and end apart: 27, of which 6 were waited for; matrix products, arithmetic and copies ran while one was open for 2% of the time, Pallas kernels for 58%

profile of v2, /device:TPU:0, one launch (start us, length us, event | category | flops | bytes accessed | tf_op | source)
XLA Modules:
  0.0 494.4 jit_solution(6315642792708709973)
XLA Ops:
  7.3 3.0 collective-permute-start.1
  11.0 2.6 multiply_convert_fusion.dm0
  13.6 1.5 collective-permute-start.5
  18.4 16.2 %collective-permute-done.1.refs_2_ = bf16[1024,512]{1,0:T(8,128)(2,1)} collective-permute-done((bf16[1024,512]{1,0:T(8,128)(2,1)}, bf16[1024,512]{1,0:T(8,128)(2,1)}, u32[]{:S(2)}, u32[]{:S(2)}) %collective-permute-start.1) | collective-permute-done | bytes 1048608 | tf_op jit(solution)/shard_map/ppermute | solution.py:39
  34.7 1.9 fusion
  38.6 11.6 %qkv.1 = (bf16[1024,2048]{1,0:T(8,128)(2,1)}, bf16[1024,2048]{1,0:T(8,128)(2,1)}, bf16[1024,1536]{1,0:T(8,128)(2,1)S(1)}) custom-call(s32[5]{0:T(128)S(1)} %stack.23.s, bf16[1024,512]{1,0:T(8,128)(2,1)} %refs_0_.1, bf16[1024,512]{1,0:T(8,128)(2,1)} %collective-permute-done.refs_1_, bf16[1024,512]{1,0:T(8,128)(2,1)} %collective-permute-done.1.refs_2_, ...), custom_call_target="tpu_custom_call" | custom-call | flops 15399999488 | bytes 50400000 | tf_op jit(solution)/shard_map/qkv/pallas_call | solution.py:66
  50.3 15.2 %attention.1 = (bf16[1024,512]{1,0:T(8,128)(2,1)S(1)}, f32[1024,512]{1,0:T(8,128)S(1)}) custom-call(s32[5]{0:T(128)S(1)} %stack.23.s, bf16[1024,1536]{1,0:T(8,128)(2,1)S(1)} %get-tuple-element.51.refs_0_.refs_1_.refs_2_, bf16[1024,1536]{1,0:T(8,128)(2,1)S(1)} %get-tuple-element.51.refs_0_.refs_1_.refs_2_, ...), custom_call_target="tpu_custom_call" | custom-call | flops 18699999232 | bytes 61200000 | tf_op jit(solution)/shard_map/attention/pallas_call | solution.py:66
  66.4 1.3 copy-done.47
  67.8 90.5 %front.1 = (bf16[2048,2048]{1,0:T(8,128)(2,1)}, bf16[2048,1024]{1,0:T(8,128)(2,1)}, bf16[2048,1024]{1,0:T(8,128)(2,1)}, bf16[2048,1024]{1,0:T(8,128)(2,1)}, bf16...) custom-call(bf16[1024,512]{1,0:T(8,128)(2,1)} %copy-done.41, ...), custom_call_target="tpu_custom_call" | custom-call | flops 88000004096 | bytes 288000000 | tf_op jit(solution)/shard_map/front/pallas_call | solution.py:692
  158.4 15.1 %grad.2.refs_2_ = bf16[4,512,2048]{2,1,0:T(8,128)(2,1)} custom-call(s32[5]{0:T(128)} %copy-done.8, bf16[2048,2048]{1,0:T(8,128)(2,1)} %get-tuple-element.59.refs_0_, bf16[2048,1024]{1,0:T(8,128)(2,1)} %get-tuple-element.54.refs_1_), custom_call_target="tpu_custom_call" | custom-call | flops 15399999488 | bytes 50400000 | tf_op jit(solution)/shard_map/grad/pallas_call | solution.py:66
  173.5 14.9 %grad.3.refs_10_ = bf16[4,512,2048]{2,1,0:T(8,128)(2,1)} custom-call(s32[5]{0:T(128)} %copy-done.8, bf16[2048,2048]{1,0:T(8,128)(2,1)} %get-tuple-element.59.refs_0_, bf16[2048,1024]{1,0:T(8,128)(2,1)} %get-tuple-element.55.refs_1_, bf16[4,512,2048]{2,1,0:T(8,128)(2,1)} %grad.2.refs_2_), custom_call_target="tpu_custom_call", output_to_operand_aliasing={{}: (3, {})} | custom-call | flops 15399999488 | bytes 50400000 | tf_op jit(solution)/shard_map/grad/pallas_call | solution.py:66
  188.5 98.5 %dn2_sum.1 = (bf16[1024,2048]{1,0:T(8,128)(2,1)}, f32[256,2048]{1,0:T(8,128)}, f32[1,2048]{1,0:T(1,128)}, f32[256,2048]{1,0:T(8,128)}, bf16[256,2048]{1,0:T(8,128)(2,1)}, /*index=5*/bf16[256,2048]{1,0:T(8,128)(2,1)}) custom-call(bf16[4,2,256,1024]{3,2,1,0:T(8,128)(2,1)} %bitcast.41, bf16[4,2,256,1024]{3,2,1,0:T(8,128)(2,1)} %bitcast.42, ...), custom_call_target="tpu_custom_call" | custom-call | flops 104500002816 | bytes 342000000 | tf_op jit(solution)/shard_map/dn2_sum/pallas_call | solution.py:921
  287.0 1.6 copy-done.14
  288.6 2.2 copy-done.38
  290.8 3.1 dob.1.refs_2_.refs_4_
  294.9 5.5 %pair_grad_send.3.refs_10_ = bf16[4,256,512]{2,1,0:T(8,128)(2,1)} custom-call(s32[5]{0:T(128)} %copy-done.8, bf16[1024,2048]{1,0:T(8,128)(2,1)} %get-tuple-element.63.refs_0_, bf16[1024,512]{1,0:T(8,128)(2,1)} %copy-done.41, bf16[1024,512]{1,0:T(8,128)(2,1)} %copy-done.42), custom_call_target="tpu_custom_call" | custom-call | flops 5500000256 | bytes 18000000 | tf_op jit(solution)/shard_map/pair_grad_send/pallas_call | solution.py:66
  300.9 13.8 %attention_back.2 = (bf16[1024,256]{1,0:T(8,128)(2,1)}, bf16[1024,256]{1,0:T(8,128)(2,1)}, bf16[1024,256]{1,0:T(8,128)(2,1)}) custom-call(s32[5]{0:T(128)} %copy-done.8, bf16[1024,1536]{1,0:T(8,128)(2,1)} %copy-done.43, bf16[1024,1536]{1,0:T(8,128)(2,1)} %copy-done.43, bf16[1024,1536]{1,0:T(8,128)(2,1)} %copy-done.43, bf16[1024,512]{1,0:T(8,128)(2,1)} %copy-done.41, ...), custom_call_target="tpu_custom_call" | custom-call | flops 14300000256 | bytes 46800000 | tf_op jit(solution)/shard_map/attention_back/pallas_call | solution.py:66
  314.7 6.5 %pair_grad_send.4.refs_1_ = bf16[4,256,768]{2,1,0:T(8,128)(2,1)} custom-call(s32[5]{0:T(128)} %copy-done.8, bf16[1024,2048]{1,0:T(8,128)(2,1)} %get-tuple-element.62.refs_0_, bf16[1024,256]{1,0:T(8,128)(2,1)} %get-tuple-element.65.refs_1_.refs_0_, bf16[1024,256]{1,0:T(8,128)(2,1)} %get-tuple-element.66.refs_2_.refs_1_, ...), custom_call_target="tpu_custom_call" | custom-call | flops 5500000256 | bytes 18000000 | tf_op jit(solution)/shard_map/pair_grad_send/pallas_call | solution.py:66
  321.1 1.5 collective-permute-start.9
  322.7 1.4 copy-done.20
  325.7 14.2 %attention_back.3 = (bf16[1024,256]{1,0:T(8,128)(2,1)}, bf16[1024,256]{1,0:T(8,128)(2,1)}, bf16[1024,256]{1,0:T(8,128)(2,1)}) custom-call(s32[5]{0:T(128)} %copy-done.8, bf16[1024,1536]{1,0:T(8,128)(2,1)} %copy-done.43, bf16[1024,1536]{1,0:T(8,128)(2,1)} %copy-done.43, bf16[1024,1536]{1,0:T(8,128)(2,1)} %copy-done.43, bf16[1024,512]{1,0:T(8,128)(2,1)} %copy-done.41, ...), custom_call_target="tpu_custom_call" | custom-call | flops 14300000256 | bytes 46800000 | tf_op jit(solution)/shard_map/attention_back/pallas_call | solution.py:66
  341.2 6.1 %pair_grad_send.5.refs_3_ = bf16[4,256,768]{2,1,0:T(8,128)(2,1)} custom-call(s32[5]{0:T(128)} %copy-done.8, bf16[1024,2048]{1,0:T(8,128)(2,1)} %get-tuple-element.62.refs_0_, bf16[1024,256]{1,0:T(8,128)(2,1)} %get-tuple-element.69.refs_1_.refs_3_, bf16[1024,256]{1,0:T(8,128)(2,1)} %get-tuple-element.70.refs_2_.refs_4_, ...), custom_call_target="tpu_custom_call" | custom-call | flops 5500000256 | bytes 18000000 | tf_op jit(solution)/shard_map/pair_grad_send/pallas_call | solution.py:66
  348.3 5.7 %pair_grad_keep.3.refs_5_.refs_6_ = bf16[4,256,512]{2,1,0:T(8,128)(2,1)} custom-call(s32[5]{0:T(128)} %copy-done.8, bf16[1024,2048]{1,0:T(8,128)(2,1)} %get-tuple-element.63.refs_0_, bf16[1024,512]{1,0:T(8,128)(2,1)} %copy-done.41, bf16[4,256,512]{2,1,0:T(8,128)(2,1)} %copy-done.55, bf16[4,256,768]{2,1,0:T(8,128)(2,1)} %pair_grad_send.5.refs_3_), custom_call_target="tpu_custom_call" | custom-call | flops 5500000256 | bytes 18000000 | tf_op jit(solution)/shard_map/pair_grad_keep/pallas_call | solution.py:66
  354.0 6.3 %collective-permute-done.9.refs_4_ = bf16[4,256,768]{2,1,0:T(8,128)(2,1)S(1)} collective-permute-done((bf16[4,256,768]{2,1,0:T(8,128)(2,1)}, bf16[4,256,768]{2,1,0:T(8,128)(2,1)S(1)}, u32[]{:S(2)}, u32[]{:S(2)}) %collective-permute-start.9) | collective-permute-done | bytes 1572896 | tf_op jit(solution)/shard_map/ppermute | solution.py:47
  361.4 7.0 %pair_grad_keep.4.refs_5_ = bf16[4,256,1280]{2,1,0:T(8,128)(2,1)} custom-call(s32[5]{0:T(128)} %copy-done.8, bf16[1024,2048]{1,0:T(8,128)(2,1)} %get-tuple-element.62.refs_0_, bf16[1024,256]{1,0:T(8,128)(2,1)} %get-tuple-element.65.refs_1_.refs_0_, bf16[1024,256]{1,0:T(8,128)(2,1)} %get-tuple-element.66.refs_2_.refs_1_, ...), custom_call_target="tpu_custom_call" | custom-call | flops 6600000000 | bytes 21600000 | tf_op jit(solution)/shard_map/pair_grad_keep/pallas_call | solution.py:66
  368.5 13.5 %collective-permute-done.7.refs_1_ = bf16[256,2048]{1,0:T(8,128)(2,1)} collective-permute-done((bf16[256,2048]{1,0:T(8,128)(2,1)}, bf16[256,2048]{1,0:T(8,128)(2,1)}, u32[]{:S(2)}, u32[]{:S(2)}) %collective-permute-start.7) | collective-permute-done | bytes 1048608 | tf_op jit(solution)/shard_map/ppermute | solution.py:47
  382.0 1.6 copy-done.39
  383.6 1.6 copy-done.40
  385.2 3.1 layer_rows.1
  390.4 9.1 %tensor_send.1 = (bf16[256,2048]{1,0:T(8,128)(2,1)}, bf16[256,2048]{1,0:T(8,128)(2,1)}) custom-call(s32[5]{0:T(128)} %copy-done.8, bf16[1024,256]{1,0:T(8,128)(2,1)} %get-tuple-element.65.refs_1_.refs_0_, bf16[1024,256]{1,0:T(8,128)(2,1)} %get-tuple-element.66.refs_2_.refs_1_, bf16[1024,256]{1,0:T(8,128)(2,1)} %get-tuple-element.67.refs_3_.refs_2_, ...), custom_call_target="tpu_custom_call" | custom-call | flops 7699999744 | bytes 25200000 | tf_op jit(solution)/shard_map/tensor_send/pallas_call | solution.py:66
  403.5 6.9 %tensor_far.1.refs_1_ = bf16[256,2048]{1,0:T(8,128)(2,1)} custom-call(s32[5]{0:T(128)} %copy-done.8, bf16[1024,256]{1,0:T(8,128)(2,1)} %get-tuple-element.65.refs_1_.refs_0_, bf16[1024,256]{1,0:T(8,128)(2,1)} %get-tuple-element.66.refs_2_.refs_1_, bf16[1024,256]{1,0:T(8,128)(2,1)} %get-tuple-element.67.refs_3_.refs_2_, ...), custom_call_target="tpu_custom_call" | custom-call | flops 7699999744 | bytes 25200000 | tf_op jit(solution)/shard_map/tensor_far/pallas_call | solution.py:66
  410.4 1.2 copy-done.21
  412.8 1.4 pair_send.2.refs_1_
  414.2 1.6 copy-done.18
  419.5 2.7 place.2.refs_13_
  422.2 7.1 %tensor_near.1.refs_5_.refs_0_ = f32[256,2048]{1,0:T(8,128)} custom-call(s32[5]{0:T(128)} %copy-done.8, bf16[1024,256]{1,0:T(8,128)(2,1)} %get-tuple-element.65.refs_1_.refs_0_, bf16[1024,256]{1,0:T(8,128)(2,1)} %get-tuple-element.66.refs_2_.refs_1_, bf16[1024,256]{1,0:T(8,128)(2,1)} %get-tuple-element.67.refs_3_.refs_2_, ...), custom_call_target="tpu_custom_call" | custom-call | flops 7699999744 | bytes 25200000 | tf_op jit(solution)/shard_map/tensor_near/pallas_call | solution.py:66
  429.3 7.9 %collective-permute-done.17.refs_4_ = bf16[4,256,768]{2,1,0:T(8,128)(2,1)} collective-permute-done((bf16[4,256,768]{2,1,0:T(8,128)(2,1)}, bf16[4,256,768]{2,1,0:T(8,128)(2,1)}, u32[]{:S(2)}, u32[]{:S(2)}) %collective-permute-start.17) | collective-permute-done | bytes 1572896 | tf_op jit(solution)/shard_map/ppermute | solution.py:47
  437.2 6.4 %pair_grad_keep.5.refs_5_ = bf16[4,256,768]{2,1,0:T(8,128)(2,1)} custom-call(s32[5]{0:T(128)} %copy-done.8, bf16[1024,2048]{1,0:T(8,128)(2,1)} %get-tuple-element.62.refs_0_, bf16[1024,256]{1,0:T(8,128)(2,1)} %get-tuple-element.69.refs_1_.refs_3_, bf16[1024,256]{1,0:T(8,128)(2,1)} %get-tuple-element.70.refs_2_.refs_4_, ...), custom_call_target="tpu_custom_call" | custom-call | flops 5500000256 | bytes 18000000 | tf_op jit(solution)/shard_map/pair_grad_keep/pallas_call | solution.py:66
  443.7 6.3 %norm1_back.1 = (bf16[256,512]{1,0:T(8,128)(2,1)}, bf16[256,512]{1,0:T(8,128)(2,1)}, bf16[256,512]{1,0:T(8,128)(2,1)}, bf16[256,512]{1,0:T(8,128)(2,1)}, f32[1,2048]{1,0:T(1,128)}) custom-call(s32[5]{0:T(128)} %copy-done.8, f32[256,2048]{1,0:T(8,128)} %tensor_near.1.refs_5_.refs_0_, bf16[256,2048]{1,0:T(8,128)(2,1)} %collective-permute-done.16.refs_1_, ...), custom_call_target="tpu_custom_call" | custom-call | flops 6600000000 | bytes 21600000 | tf_op jit(solution)/shard_map/norm1_back/pallas_call | solution.py:66
  450.3 1.6 collective-permute-start.20
  453.6 1.5 flip.1.refs_2_
  456.2 3.0 pair_join.2.refs_0_
  459.2 1.6 copy-done.33
  460.8 15.7 %gains.1.refs_2_ = f32[2,2048]{1,0:T(2,128)S(1)} custom-call(f32[1,2048]{1,0:T(1,128)S(1)} %copy-done.49, f32[1,2048]{1,0:T(1,128)S(1)} %copy-done.50, f32[2048,256]{1,0:T(8,128)S(1)} %copy-done.33), custom_call_target="tpu_custom_call" | custom-call | flops 13200000000 | bytes 43200000 | tf_op jit(solution)/shard_map/gains/pallas_call | solution.py:1124
  477.2 2.7 pair_join.3
  480.0 1.6 copy-done.34
  481.6 1.8 place.3.refs_2_
  485.6 1.7 head_halves.1
  (173 shorter events, 30.7 us)
Async XLA Ops:
  7.2 9.0 %copy-start.57 = (s32[8]{0:T(128)S(1)}, s32[8]{0:T(128)}, u32[]{:S(2)}) copy-start(s32[8]{0:T(128)} %param.24) | copy-start | bytes 100
  7.2 9.2 %copy-start.51 = (bf16[2048]{0:T(1024)(128)(2,1)S(1)}, bf16[2048]{0:T(1024)(128)(2,1)}, u32[]{:S(2)}) copy-start(bf16[2048]{0:T(1024)(128)(2,1)} %param.14) | copy-start | bytes 12292
  7.2 9.2 %copy-start.52 = (bf16[2048]{0:T(1024)(128)(2,1)S(1)}, bf16[2048]{0:T(1024)(128)(2,1)}, u32[]{:S(2)}) copy-start(bf16[2048]{0:T(1024)(128)(2,1)} %param.19) | copy-start | bytes 12292
  7.2 403.1 %reduce-scatter.7.cloned.1.call-start = ((), (), s32[]{:S(2)}) async-start(), calls=%async_computation.5 | async-start | bytes 5242880 | tf_op jit(solution)/shard_map/reduce_scatter | solution.py:975
  7.3 27.3 %collective-permute-start.1 = (bf16[1024,512]{1,0:T(8,128)(2,1)}, bf16[1024,512]{1,0:T(8,128)(2,1)}, u32[]{:S(2)}, u32[]{:S(2)}) collective-permute-start(bf16[1024,512]{1,0:T(8,128)(2,1)} %refs_0_.1), channel_id=1, source_target_pairs={{0,2},{2,0},{1,3},{3,1},{4,6},{6,4},{5,7},{7,5},{8,10},{10,8},{9,1... | collective-permute-start | bytes 3145736 | tf_op jit(solution)/shard_map/ppermute | solution.py:39
  11.0 27.6 %copy-start.17 = (bf16[2048,512]{1,0:T(8,128)(2,1)S(1)}, bf16[2048,512]{1,0:T(8,128)(2,1)}, u32[]{:S(2)}) copy-start(bf16[2048,512]{1,0:T(8,128)(2,1)} %refs_11_.5) | copy-start | bytes 6291460
  13.6 24.9 %collective-permute-start.5 = (bf16[1024,512]{1,0:T(8,128)(2,1)}, bf16[1024,512]{1,0:T(8,128)(2,1)}, u32[]{:S(2)}, u32[]{:S(2)}) collective-permute-start(bf16[1024,512]{1,0:T(8,128)(2,1)} %multiply_convert_fusion.dm0), channel_id=1, source_target_pairs={{0,4},{4,0},{8,12},{12,8},{16,20},{20,16},{24,28},{28,24},{1,5},{5... | collective-permute-start | bytes 3145736 | tf_op jit(solution)/shard_map/ppermute | solution.py:47
  15.1 52.6 %collective-permute-start.4 = (bf16[1024,512]{1,0:T(8,128)(2,1)}, bf16[1024,512]{1,0:T(8,128)(2,1)}, u32[]{:S(2)}, u32[]{:S(2)}) collective-permute-start(bf16[1024,512]{1,0:T(8,128)(2,1)} %multiply_convert_fusion.dm0), channel_id=1, source_target_pairs={{0,2},{2,0},{1,3},{3,1},{4,6},{6,4},{5,7},{7,5},{8,10},{10,8},{9,1... | collective-permute-start | bytes 3145736 | tf_op jit(solution)/shard_map/ppermute | solution.py:39
  15.6 52.1 %collective-permute-start.3 = (bf16[1024,512]{1,0:T(8,128)(2,1)}, bf16[1024,512]{1,0:T(8,128)(2,1)}, u32[]{:S(2)}, u32[]{:S(2)}) collective-permute-start(bf16[1024,512]{1,0:T(8,128)(2,1)} %multiply_convert_fusion.dm0), channel_id=1, source_target_pairs={{0,1},{1,0},{2,3},{3,2},{4,5},{5,4},{6,7},{7,6},{8,9},{9,8},{10,11... | collective-permute-start | bytes 3145736 | tf_op jit(solution)/shard_map/ppermute | solution.py:35
  15.6 22.9 %collective-permute-start = (bf16[1024,512]{1,0:T(8,128)(2,1)}, bf16[1024,512]{1,0:T(8,128)(2,1)}, u32[]{:S(2)}, u32[]{:S(2)}) collective-permute-start(bf16[1024,512]{1,0:T(8,128)(2,1)} %refs_0_.1), channel_id=1, source_target_pairs={{0,1},{1,0},{2,3},{3,2},{4,5},{5,4},{6,7},{7,6},{8,9},{9,8},{10,11... | collective-permute-start | bytes 3145736 | tf_op jit(solution)/shard_map/ppermute | solution.py:35
  16.4 22.2 %copy-start.6 = (bf16[1,2048]{1,0:T(2,128)(2,1)}, bf16[1,2048]{1,0:T(2,128)(2,1)S(1)}, u32[]{:S(2)}) copy-start(bf16[1,2048]{1,0:T(2,128)(2,1)S(1)} %broadcast_in_dim.9.refs_4_.refs_3_) | copy-start | bytes 12292
  18.3 31.9 %copy-start.5 = (s32[1024,1]{1,0:T(8,128)}, s32[1024,1]{1,0:T(8,128)S(1)}, u32[]{:S(2)}) copy-start(s32[1024,1]{1,0:T(8,128)S(1)} %copy.32.refs_3_.refs_6_) | copy-start | bytes 12292
  18.4 31.8 %copy-start.8 = (s32[5]{0:T(128)}, s32[5]{0:T(128)S(1)}, u32[]{:S(2)}) copy-start(s32[5]{0:T(128)S(1)} %stack.23.s) | copy-start | bytes 64
  34.6 4.0 collective-permute-start.2
  37.5 12.7 %copy-start.2 = (f32[1024,128]{1,0:T(8,128)}, f32[1024,128]{1,0:T(8,128)S(1)}, u32[]{:S(2)}) copy-start(f32[1024,128]{1,0:T(8,128)S(1)} %get-tuple-element.98.refs_8_) | copy-start | bytes 1572868
  37.5 12.7 %copy-start.3 = (f32[1024,128]{1,0:T(8,128)}, f32[1024,128]{1,0:T(8,128)S(1)}, u32[]{:S(2)}) copy-start(f32[1024,128]{1,0:T(8,128)S(1)} %get-tuple-element.99.refs_9_) | copy-start | bytes 1572868
  37.6 12.7 %copy-start.7 = (s32[8,128]{1,0:T(8,128)}, s32[8,128]{1,0:T(8,128)S(1)}, u32[]{:S(2)}) copy-start(s32[8,128]{1,0:T(8,128)S(1)} %fusion.2) | copy-start | bytes 12292
  38.6 29.2 %collective-permute-start.6 = (bf16[1024,512]{1,0:T(8,128)(2,1)}, bf16[1024,512]{1,0:T(8,128)(2,1)}, u32[]{:S(2)}, u32[]{:S(2)}) collective-permute-start(bf16[1024,512]{1,0:T(8,128)(2,1)} %collective-permute-done.5.dmx), channel_id=1, source_target_pairs={{0,1},{1,0},{2,3},{3,2},{4,5},{5,4},{6,7},{7,6},{8,9},{9,8},{10,11... | collective-permute-start | bytes 3145736 | tf_op jit(solution)/shard_map/ppermute | solution.py:35
  50.2 15.2 %copy-start.43 = (bf16[1024,1536]{1,0:T(8,128)(2,1)}, bf16[1024,1536]{1,0:T(8,128)(2,1)S(1)}, u32[]{:S(2)}) copy-start(bf16[1024,1536]{1,0:T(8,128)(2,1)S(1)} %get-tuple-element.51.refs_0_.refs_1_.refs_2_) | copy-start | bytes 9437188
  158.3 255.9 %reduce-scatter.5.cloned.1.call-start = ((), (), s32[]{:S(2)}) async-start(), calls=%async_computation.4 | async-start | bytes 10485760 | tf_op jit(solution)/shard_map/reduce_scatter | solution.py:975
  188.4 263.4 %reduce-scatter.9.cloned.1.call-start = ((), (), s32[]{:S(2)}) async-start(), calls=%async_computation.6 | async-start | bytes 3276800 | tf_op jit(solution)/shard_map/reduce_scatter | solution.py:975
  188.5 98.5 %copy-start.9 = (s32[5]{0:T(128)S(1)}, s32[5]{0:T(128)}, u32[]{:S(2)}) copy-start(s32[5]{0:T(128)} %copy-done.8) | copy-start | bytes 64
  300.4 47.0 %collective-permute-start.10 = (bf16[4,256,512]{2,1,0:T(8,128)(2,1)}, bf16[4,256,512]{2,1,0:T(8,128)(2,1)S(1)}, u32[]{:S(2)}, u32[]{:S(2)}) collective-permute-start(bf16[4,256,512]{2,1,0:T(8,128)(2,1)} %pair_grad_send.3.refs_10_), channel_id=1, source_target_pairs={{0,4},{4,0},{8,12},{12,8},{16,20},{20,16},{24,28},{28,24},{1,5},{5... | collective-permute-start | bytes 3145736 | tf_op jit(solution)/shard_map/ppermute | solution.py:47
  314.7 8.0 %copy-start.10 = (s32[5]{0:T(128)S(1)}, s32[5]{0:T(128)}, u32[]{:S(2)}) copy-start(s32[5]{0:T(128)} %copy-done.8) | copy-start | bytes 64
  314.7 8.0 %copy-start.37 = (bf16[256,2048]{1,0:T(8,128)(2,1)S(1)}, bf16[256,2048]{1,0:T(8,128)(2,1)}, u32[]{:S(2)}) copy-start(bf16[256,2048]{1,0:T(8,128)(2,1)} %get-tuple-element.61.refs_0_) | copy-start | bytes 3145732
  321.1 39.2 %collective-permute-start.9 = (bf16[4,256,768]{2,1,0:T(8,128)(2,1)}, bf16[4,256,768]{2,1,0:T(8,128)(2,1)S(1)}, u32[]{:S(2)}, u32[]{:S(2)}) collective-permute-start(bf16[4,256,768]{2,1,0:T(8,128)(2,1)} %pair_grad_send.4.refs_1_), channel_id=1, source_target_pairs={{0,4},{4,0},{8,12},{12,8},{16,20},{20,16},{24,28},{28,24},{1,5},{5... | collective-permute-start | bytes 4718600 | tf_op jit(solution)/shard_map/ppermute | solution.py:47
  339.9 42.2 %collective-permute-start.7 = (bf16[256,2048]{1,0:T(8,128)(2,1)}, bf16[256,2048]{1,0:T(8,128)(2,1)}, u32[]{:S(2)}, u32[]{:S(2)}) collective-permute-start(bf16[256,2048]{1,0:T(8,128)(2,1)} %copy-done.25), channel_id=1, source_target_pairs={{0,4},{4,0},{8,12},{12,8},{16,20},{20,16},{24,28},{28,24},{1,5},{5... | collective-permute-start | bytes 3145736 | tf_op jit(solution)/shard_map/ppermute | solution.py:47
  340.4 28.1 %collective-permute-start.8 = (bf16[256,2048]{1,0:T(8,128)(2,1)}, bf16[256,2048]{1,0:T(8,128)(2,1)}, u32[]{:S(2)}, u32[]{:S(2)}) collective-permute-start(bf16[256,2048]{1,0:T(8,128)(2,1)} %get-tuple-element.68), channel_id=1, source_target_pairs={{0,2},{2,0},{1,3},{3,1},{4,6},{6,4},{5,7},{7,5},{8,10},{10,8},{9,1... | collective-permute-start | bytes 3145736 | tf_op jit(solution)/shard_map/ppermute | solution.py:39
  361.4 20.6 %copy-start.4 = (f32[1024,1]{1,0:T(8,128)S(1)}, f32[1024,1]{1,0:T(8,128)}, u32[]{:S(2)}) copy-start(f32[1024,1]{1,0:T(8,128)} %copy.33.live.refs_8_.refs_4_) | copy-start | bytes 12292
  368.4 13.6 %copy-start = (bf16[4,256,1280]{2,1,0:T(8,128)(2,1)S(1)}, bf16[4,256,1280]{2,1,0:T(8,128)(2,1)}, u32[]{:S(2)}) copy-start(bf16[4,256,1280]{2,1,0:T(8,128)(2,1)} %pair_grad_keep.4.refs_5_) | copy-start | bytes 7864324
  368.4 13.6 %copy-start.11 = (s32[5]{0:T(128)S(1)}, s32[5]{0:T(128)}, u32[]{:S(2)}) copy-start(s32[5]{0:T(128)} %copy-done.8) | copy-start | bytes 64
  368.5 114.9 %reduce-scatter.11.cloned.1.call-start = ((), (), s32[]{:S(2)}) async-start(), calls=%async_computation.7 | async-start | bytes 1966080 | tf_op jit(solution)/shard_map/reduce_scatter | solution.py:975
  390.4 9.3 %copy-start.32 = (bf16[256,512]{1,0:T(8,128)(2,1)S(1)}, bf16[256,512]{1,0:T(8,128)(2,1)}, u32[]{:S(2)}) copy-start(bf16[256,512]{1,0:T(8,128)(2,1)} %copy-done.31) | copy-start | bytes 786436
  390.4 9.7 %copy-start.30 = (bf16[256,512]{1,0:T(8,128)(2,1)S(1)}, bf16[256,512]{1,0:T(8,128)(2,1)}, u32[]{:S(2)}) copy-start(bf16[256,512]{1,0:T(8,128)(2,1)} %copy-done.29) | copy-start | bytes 786436
  399.6 2.9 collective-permute-start.14
  399.6 37.6 %collective-permute-start.17 = (bf16[4,256,768]{2,1,0:T(8,128)(2,1)}, bf16[4,256,768]{2,1,0:T(8,128)(2,1)}, u32[]{:S(2)}, u32[]{:S(2)}) collective-permute-start(bf16[4,256,768]{2,1,0:T(8,128)(2,1)} %pair_grad_send.5.refs_3_), channel_id=1, source_target_pairs={{0,4},{4,0},{8,12},{12,8},{16,20},{20,16},{24,28},{28,24},{1,5},{5... | collective-permute-start | bytes 4718600 | tf_op jit(solution)/shard_map/ppermute | solution.py:47
  399.7 16.8 %collective-permute-start.11 = (bf16[256,512]{1,0:T(8,128)(2,1)S(1)}, bf16[256,512]{1,0:T(8,128)(2,1)}, u32[]{:S(2)}, u32[]{:S(2)}) collective-permute-start(bf16[256,512]{1,0:T(8,128)(2,1)S(1)} %copy-done.32), channel_id=1, source_target_pairs={{0,1},{1,0},{2,3},{3,2},{4,5},{5,4},{6,7},{7,6},{8,9},{9,8},{10,11... | collective-permute-start | bytes 786440 | tf_op jit(solution)/shard_map/ppermute | solution.py:35
  400.1 17.3 %collective-permute-start.12 = (bf16[256,512]{1,0:T(8,128)(2,1)S(1)}, bf16[256,512]{1,0:T(8,128)(2,1)}, u32[]{:S(2)}, u32[]{:S(2)}) collective-permute-start(bf16[256,512]{1,0:T(8,128)(2,1)S(1)} %copy-done.30), channel_id=1, source_target_pairs={{0,2},{2,0},{1,3},{3,1},{4,6},{6,4},{5,7},{7,5},{8,10},{10,8},{9,1... | collective-permute-start | bytes 786440 | tf_op jit(solution)/shard_map/ppermute | solution.py:39
  400.7 17.9 %collective-permute-start.13 = (bf16[256,512]{1,0:T(8,128)(2,1)S(1)}, bf16[256,512]{1,0:T(8,128)(2,1)}, u32[]{:S(2)}, u32[]{:S(2)}) collective-permute-start(bf16[256,512]{1,0:T(8,128)(2,1)S(1)} %get-tuple-element.75), channel_id=1, source_target_pairs={{0,3},{3,0},{1,2},{2,1},{4,7},{7,4},{5,6},{6,5},{8,11},{11,8},{9,1... | collective-permute-start | bytes 786440 | tf_op jit(solution)/shard_map/ppermute | solution.py:43
  402.5 19.7 %collective-permute-start.15 = (bf16[256,2048]{1,0:T(8,128)(2,1)}, bf16[256,2048]{1,0:T(8,128)(2,1)}, u32[]{:S(2)}, u32[]{:S(2)}) collective-permute-start(bf16[256,2048]{1,0:T(8,128)(2,1)} %get-tuple-element.78), channel_id=1, source_target_pairs={{0,1},{1,0},{2,3},{3,2},{4,5},{5,4},{6,7},{7,6},{8,9},{9,8},{10,11... | collective-permute-start | bytes 3145736 | tf_op jit(solution)/shard_map/ppermute | solution.py:35
  417.1 26.6 %collective-permute-start.16 = (bf16[256,2048]{1,0:T(8,128)(2,1)S(1)}, bf16[256,2048]{1,0:T(8,128)(2,1)}, u32[]{:S(2)}, u32[]{:S(2)}) collective-permute-start(bf16[256,2048]{1,0:T(8,128)(2,1)S(1)} %copy-done.24), channel_id=1, source_target_pairs={{0,2},{2,0},{1,3},{3,1},{4,6},{6,4},{5,7},{7,5},{8,10},{10,8},{9,1... | collective-permute-start | bytes 3145736 | tf_op jit(solution)/shard_map/ppermute | solution.py:39
  417.4 37.7 %collective-permute-start.22 = (bf16[1024,256]{1,0:T(8,128)(2,1)}, bf16[1024,256]{1,0:T(8,128)(2,1)}, u32[]{:S(2)}, u32[]{:S(2)}) collective-permute-start(bf16[1024,256]{1,0:T(8,128)(2,1)} %pair_send.2.refs_1_), channel_id=1, source_target_pairs={{0,4},{4,0},{8,12},{12,8},{16,20},{20,16},{24,28},{28,24},{1,5},{5... | collective-permute-start | bytes 1572872 | tf_op jit(solution)/shard_map/ppermute | solution.py:47
  418.6 58.6 %collective-permute-start.21 = (bf16[256,2048]{1,0:T(8,128)(2,1)S(1)}, bf16[256,2048]{1,0:T(8,128)(2,1)S(1)}, u32[]{:S(2)}, u32[]{:S(2)}) collective-permute-start(bf16[256,2048]{1,0:T(8,128)(2,1)S(1)} %pair_send.3.refs_4_), channel_id=1, source_target_pairs={{0,4},{4,0},{8,12},{12,8},{16,20},{20,16},{24,28},{28,24},{1,5},{5... | collective-permute-start | bytes 3145736 | tf_op jit(solution)/shard_map/ppermute | solution.py:47
  443.7 8.2 %copy-start.13 = (s32[5]{0:T(128)S(1)}, s32[5]{0:T(128)}, u32[]{:S(2)}) copy-start(s32[5]{0:T(128)} %copy-done.8) | copy-start | bytes 64
  450.0 30.0 %collective-permute-start.18 = (bf16[256,512]{1,0:T(8,128)(2,1)}, bf16[256,512]{1,0:T(8,128)(2,1)S(1)}, u32[]{:S(2)}, u32[]{:S(2)}) collective-permute-start(bf16[256,512]{1,0:T(8,128)(2,1)} %get-tuple-element.81), channel_id=1, source_target_pairs={{0,1},{1,0},{2,3},{3,2},{4,5},{5,4},{6,7},{7,6},{8,9},{9,8},{10,11... | collective-permute-start | bytes 786440 | tf_op jit(solution)/shard_map/ppermute | solution.py:35
  450.0 30.0 %collective-permute-start.19 = (bf16[256,512]{1,0:T(8,128)(2,1)}, bf16[256,512]{1,0:T(8,128)(2,1)S(1)}, u32[]{:S(2)}, u32[]{:S(2)}) collective-permute-start(bf16[256,512]{1,0:T(8,128)(2,1)} %get-tuple-element.82), channel_id=1, source_target_pairs={{0,2},{2,0},{1,3},{3,1},{4,6},{6,4},{5,7},{7,5},{8,10},{10,8},{9,1... | collective-permute-start | bytes 786440 | tf_op jit(solution)/shard_map/ppermute | solution.py:39
  450.3 29.7 %collective-permute-start.20 = (bf16[256,512]{1,0:T(8,128)(2,1)}, bf16[256,512]{1,0:T(8,128)(2,1)S(1)}, u32[]{:S(2)}, u32[]{:S(2)}) collective-permute-start(bf16[256,512]{1,0:T(8,128)(2,1)} %get-tuple-element.83), channel_id=1, source_target_pairs={{0,3},{3,0},{1,2},{2,1},{4,7},{7,4},{5,6},{6,5},{8,11},{11,8},{9,1... | collective-permute-start | bytes 786440 | tf_op jit(solution)/shard_map/ppermute | solution.py:43
  460.8 16.4 %copy-start.19 = (bf16[1,512,2048]{2,1,0:T(8,128)(2,1)S(1)}, bf16[1,512,2048]{2,1,0:T(8,128)(2,1)}, u32[]{:S(2)}) copy-start(bf16[1,512,2048]{2,1,0:T(8,128)(2,1)} %reduce-scatter.5.cloned.1.call-done) | copy-start | bytes 6291460
  (37 other events, 68.5 us)
Sparse Core Ops, SparseCore 0:
  158.5 77.7 reduce-scatter.6
  238.7 144.9 reduce-scatter.4
  386.1 52.8 reduce-scatter.8
  443.8 35.5 reduce-scatter.10
